TPU v7x, 32 devices: a whole 2x2x4 slice. The times are simulated.
32 devices in a mesh: dp: 16 (over z, y, core), tensor: 2 (over x).
Axes of the slice: x: 2, y: 2, z: 4, core: 2. Of those that a mesh axis runs over, the one named last changes fastest.
Arguments:
- queries: bfloat16 [32, 256, 8192], P('dp', None, 'tensor'), may hold values from -5 to 5
- resp_kv: bfloat16 [32, 256, 2, 1024], P('dp', None, None, 'tensor'), may hold values from -12 to 12
- prefix_pool: bfloat16 [512, 2, 2, 1024], P(('dp', 'tensor')), may hold values from -12 to 12
- grad_out: bfloat16 [32, 256, 8192], P('dp', None, 'tensor'), may hold values from -12 to 12
- member_list: int32 [2, 8], replicated, may hold values from 0 to 15, as said below
- prompt_slot: int32 [2], replicated, may hold values from 0 to 1, each once
- resp_len: int32 [32], P('dp'), may hold values from 1 to 256, 5120 in all
Outputs:
- attention: bfloat16 [32, 256, 8192], P('dp', None, 'tensor')
- grad_queries: bfloat16 [32, 256, 8192], P('dp', None, 'tensor')
- grad_resp_kv: bfloat16 [32, 256, 2, 1024], P('dp', None, None, 'tensor')
- grad_prefix: bfloat16 [512, 2, 2, 1024], P(('dp', 'tensor'))
Inputs may be any that keep to these rules, and one draw needn't show every extreme that they name: `member_list`: each dp index appears exactly once.
All inputs are finite; a program needn't handle non-finite values. No bound on the sum of `resp_len` on one device may be relied on, other than what follows from the above.
Results may differ from a plain program's by a relative error of at most 0.024.
Values may be sent and summed in bfloat16 or wider, within the bound.
No kernel may reach another device: no remote copies, remote signals or barrier semaphores. Data moves between devices by JAX's collectives and lax.ppermute only.
A program may use at most 128 MiB of HBM per device.

v0:
```python
import math

import jax
import jax.numpy as jnp
from jax import lax
from jax.sharding import PartitionSpec as P

HEAD_SIZE = 128
PROMPT_LENGTH = 512


def on_device(queries, resp_kv, prefix_pool, grad_out, member_list, prompt_slot, resp_len):
    dp_count = lax.axis_size("dp")
    tensor_count = lax.axis_size("tensor")
    dp_index = lax.axis_index("dp")
    head_dim = HEAD_SIZE
    responses = queries.shape[0]
    row_count = queries.shape[1]
    kv_local = resp_kv.shape[3] // head_dim
    heads_local = queries.shape[2] // head_dim
    heads_per_group = heads_local // kv_local
    prompt_count = member_list.shape[0]
    slice_rows = prefix_pool.shape[0]
    kv_total = kv_local * tensor_count
    score_scale = head_dim ** (-0.5)
    owner_hit = member_list[:, :, None] == jnp.arange(dp_count, dtype=jnp.int32)[None, None, :]
    prompt_of = jnp.sum(
        jnp.where(owner_hit, jnp.arange(prompt_count, dtype=jnp.int32)[:, None, None], 0),
        axis=(0, 1),
    )
    prompt_hot = (prompt_of[:, None] == jnp.arange(prompt_count, dtype=jnp.int32)[None, :]).astype(
        jnp.int32
    )
    slot_of = jnp.sum(prompt_hot * prompt_slot[None, :], axis=1)
    slot_hot = slot_of[:, None] == jnp.arange(prompt_count, dtype=jnp.int32)[None, :]
    mine_hot = lax.dynamic_index_in_dim(slot_hot, dp_index, 0, keepdims=False)
    my_slot = lax.dynamic_index_in_dim(slot_of, dp_index, 0, keepdims=False)
    regrouped = lax.all_to_all(
        prefix_pool.reshape(1, slice_rows, prompt_count, 2, kv_total, head_dim),
        "tensor",
        split_axis=4,
        concat_axis=0,
        tiled=True,
    )
    regrouped = regrouped.reshape(tensor_count * slice_rows, prompt_count, 2, kv_local * head_dim)
    picked = lax.dynamic_index_in_dim(
        lax.all_gather(regrouped, "dp", axis=0, tiled=True), my_slot, 1, keepdims=False
    )
    prefix_mine = picked
    prefix_kv = prefix_mine.reshape(PROMPT_LENGTH, 2, kv_local, head_dim)
    query_five = queries.reshape(responses, row_count, kv_local, heads_per_group, head_dim)
    live_rows = jnp.arange(row_count, dtype=jnp.int32)[None, :] < resp_len[:, None]
    live_float = live_rows.astype(jnp.float32)
    active_gradient = (
        grad_out.reshape(responses, row_count, kv_local, heads_per_group, head_dim)
        * live_rows.astype(jnp.bfloat16)[:, :, None, None, None]
    )
    own_all = resp_kv.reshape(responses, row_count, 2, kv_local, head_dim)
    head_block = math.gcd(heads_per_group, max(1, 1024 // (responses * row_count)))
    per_kv = heads_per_group // head_block
    causal = jnp.arange(row_count)[None, :] <= jnp.arange(row_count)[:, None]

    def attend(step_index, carry_state):
        attn_buf, dq_buf, prefix_grad, own_grad = carry_state
        kv_head = step_index // per_kv
        first_head = step_index % per_kv * head_block
        corner = (0, 0, kv_head, first_head, 0)
        extent = (responses, row_count, 1, head_block, head_dim)
        query_block = lax.dynamic_slice(query_five, corner, extent)[:, :, 0]
        grad_block = lax.dynamic_slice(active_gradient, corner, extent)[:, :, 0]
        prefix_head = lax.dynamic_index_in_dim(prefix_kv, kv_head, 2, keepdims=False)
        own_kv = lax.dynamic_index_in_dim(own_all, kv_head, 3, keepdims=False)
        far_score = (
            jnp.einsum(
                "rseh,jh->resj", query_block, prefix_head[:, 0], preferred_element_type=jnp.float32
            )
            * score_scale
        )
        near_score = (
            jnp.einsum(
                "rseh,rth->rest", query_block, own_kv[:, :, 0], preferred_element_type=jnp.float32
            )
            * score_scale
        )
        near_score = jnp.where(causal[None, None], near_score, -jnp.inf)
        row_peak = jnp.maximum(jnp.max(far_score, axis=-1), jnp.max(near_score, axis=-1))[..., None]
        far_exp = jnp.exp(far_score - row_peak)
        near_exp = jnp.exp(near_score - row_peak)
        row_total = jnp.sum(far_exp, axis=-1, keepdims=True) + jnp.sum(
            near_exp, axis=-1, keepdims=True
        )
        far_prob = far_exp / row_total
        near_prob = near_exp / row_total
        far_b = far_prob.astype(jnp.bfloat16)
        near_b = near_prob.astype(jnp.bfloat16)
        attended = jnp.einsum(
            "resj,jh->rseh", far_b, prefix_head[:, 1], preferred_element_type=jnp.float32
        )
        attended = attended + jnp.einsum(
            "rest,rth->rseh", near_b, own_kv[:, :, 1], preferred_element_type=jnp.float32
        )
        block_out = (attended * live_float[:, :, None, None]).astype(jnp.bfloat16)
        row_delta = jnp.einsum(
            "rseh,rseh->res", grad_block, block_out, preferred_element_type=jnp.float32
        )
        far_dprob = jnp.einsum(
            "rseh,jh->resj", grad_block, prefix_head[:, 1], preferred_element_type=jnp.float32
        )
        near_dprob = jnp.einsum(
            "rseh,rth->rest", grad_block, own_kv[:, :, 1], preferred_element_type=jnp.float32
        )
        far_ds = (far_prob * (far_dprob - row_delta[..., None])).astype(jnp.bfloat16)
        near_ds = (near_prob * (near_dprob - row_delta[..., None])).astype(jnp.bfloat16)
        grad_query = jnp.einsum(
            "resj,jh->rseh", far_ds, prefix_head[:, 0], preferred_element_type=jnp.float32
        )
        grad_query = grad_query + jnp.einsum(
            "rest,rth->rseh", near_ds, own_kv[:, :, 0], preferred_element_type=jnp.float32
        )
        grad_query = (grad_query * score_scale).astype(jnp.bfloat16)
        far_dk = (
            jnp.einsum("resj,rseh->jh", far_ds, query_block, preferred_element_type=jnp.float32)
            * score_scale
        )
        far_dv = jnp.einsum("resj,rseh->jh", far_b, grad_block, preferred_element_type=jnp.float32)
        near_dk = (
            jnp.einsum("rest,rseh->rth", near_ds, query_block, preferred_element_type=jnp.float32)
            * score_scale
        )
        near_dv = jnp.einsum(
            "rest,rseh->rth", near_b, grad_block, preferred_element_type=jnp.float32
        )
        attn_buf = lax.dynamic_update_slice(attn_buf, block_out[:, :, None], corner)
        dq_buf = lax.dynamic_update_slice(dq_buf, grad_query[:, :, None], corner)
        prefix_corner = (0, 0, kv_head, 0)
        prefix_now = lax.dynamic_slice(prefix_grad, prefix_corner, (PROMPT_LENGTH, 2, 1, head_dim))
        prefix_grad = lax.dynamic_update_slice(
            prefix_grad, prefix_now + jnp.stack([far_dk, far_dv], axis=1)[:, :, None], prefix_corner
        )
        own_corner = (0, 0, 0, kv_head, 0)
        own_now = lax.dynamic_slice(own_grad, own_corner, (responses, row_count, 2, 1, head_dim))
        own_grad = lax.dynamic_update_slice(
            own_grad, own_now + jnp.stack([near_dk, near_dv], axis=2)[:, :, :, None], own_corner
        )
        return (attn_buf, dq_buf, prefix_grad, own_grad)

    start_state = (
        jnp.zeros((responses, row_count, kv_local, heads_per_group, head_dim), dtype=jnp.bfloat16),
        jnp.zeros((responses, row_count, kv_local, heads_per_group, head_dim), dtype=jnp.bfloat16),
        jnp.zeros((PROMPT_LENGTH, 2, kv_local, head_dim), dtype=jnp.float32),
        jnp.zeros((responses, row_count, 2, kv_local, head_dim), dtype=jnp.float32),
    )
    attn_buf, dq_buf, prefix_grad, own_grad = lax.fori_loop(
        0, kv_local * per_kv, attend, start_state
    )
    attention = attn_buf.reshape(responses, row_count, heads_local * head_dim)
    grad_queries = dq_buf.reshape(responses, row_count, heads_local * head_dim)
    grad_resp_kv = own_grad.reshape(responses, row_count, 2, kv_local * head_dim).astype(
        jnp.bfloat16
    )
    prefix_flat = prefix_grad.reshape(PROMPT_LENGTH, 2, kv_local * head_dim)
    mine_float = mine_hot.astype(jnp.float32)
    picked = prefix_flat
    summed = lax.psum_scatter(
        picked[:, None] * mine_float[None, :, None, None], "dp", scatter_dimension=0, tiled=True
    )
    summed = summed.astype(jnp.bfloat16).reshape(
        tensor_count, slice_rows, prompt_count, 2, kv_local, head_dim
    )
    returned = lax.all_to_all(summed, "tensor", split_axis=0, concat_axis=4, tiled=True)
    grad_prefix = returned.reshape(slice_rows, prompt_count, 2, kv_total * head_dim)
    return (attention, grad_queries, grad_resp_kv, grad_prefix)


def solution(mesh):
    return jax.shard_map(
        on_device,
        mesh=mesh,
        in_specs=(
            P("dp", None, "tensor"),
            P("dp", None, None, "tensor"),
            P(("dp", "tensor"), None, None, None),
            P("dp", None, "tensor"),
            P(),
            P(),
            P("dp"),
        ),
        out_specs=(
            P("dp", None, "tensor"),
            P("dp", None, "tensor"),
            P("dp", None, None, "tensor"),
            P(("dp", "tensor"), None, None, None),
        ),
        check_vma=False,
    )
```

profile of v0, /device:TPU:1, one launch (start us, length us, event | category | flops | bytes accessed | tf_op | source)
XLA Modules:
  0.0 499.9 jit_solution(14910093035668613970)
XLA Ops:
  8.4 6.4 %all_to_all.30 = bf16[1,16,2,2,8,128]{5,1,3,2,0,4:T(8,128)(2,1)S(1)} all-to-all(bf16[1,16,2,2,8,128]{5,1,3,2,0,4:T(8,128)(2,1)S(1)} %copy.154), channel_id=1, replica_groups=mesh['dp'=16,'tensor'=2] {'tensor'}, dimensions={4} | all-to-all | bytes 262144 | tf_op jit(solution)/shard_map/all_to_all | solution.py:38
  19.1 2.2 copy.159
  21.3 6.3 %copy.158 = bf16[2,256,4096]{1,2,0:T(8,128)(2,1)} copy(bf16[2,256,4096]{2,1,0:T(8,128)(2,1)} %param.9) | data formatting | bytes 8388608 | tf_op args[0]
  27.6 6.3 %copy.160 = bf16[2,256,4096]{1,2,0:T(8,128)(2,1)} copy(bf16[2,256,4096]{2,1,0:T(8,128)(2,1)} %param.12) | data formatting | bytes 8388608 | tf_op args[3]
  35.3 4.4 broadcast_multiply_fusion.1
  39.7 19.7 %all-gather.2.cloned.1.call-done = bf16[512,2,2,512]{3,0,2,1:T(8,128)(2,1)} async-done(((bf16[32,2,2,512]{3,0,2,1:T(8,128)(2,1)}), bf16[512,2,2,512]{3,0,2,1:T(8,128)(2,1)}) %all-gather.2.cloned.1.call-update) | async-done | bytes 2097168 | tf_op jit(solution)/shard_map/all_gather | solution.py:47
  65.2 2.5 broadcast.83.clone2
  67.7 2.6 broadcast.83.clone
  70.2 325.5 %while.22 = (s32[]{:T(128)}, bf16[2,256,4,8,128]{4,3,2,1,0:T(8,128)(2,1)}, bf16[2,256,4,8,128]{4,3,2,1,0:T(8,128)(2,1)}, f32[512,2,4,128]{0,3,2,1:T(8,128)}, f32...) while((s32[]{:T(128)}, ...), condition=%wide.region_7.8_spmd.clone, body=%wide.region_2.7_spmd.clone.sunk | while | flops 1221261312 | bytes 46629340 | solution.py:153
  79.8 2.1 convolution_bitcast_fusion.15
  87.5 1.9 fusion.112
  100.2 2.1 convolution_bitcast_fusion.15
  120.6 2.1 convolution_bitcast_fusion.15
  140.9 2.1 convolution_bitcast_fusion.15
  148.6 1.9 fusion.112
  161.3 2.1 convolution_bitcast_fusion.15
  181.6 2.1 convolution_bitcast_fusion.15
  201.9 2.1 convolution_bitcast_fusion.15
  222.3 2.1 convolution_bitcast_fusion.15
  242.6 2.1 convolution_bitcast_fusion.15
  262.9 2.1 convolution_bitcast_fusion.15
  283.3 2.1 convolution_bitcast_fusion.15
  303.6 2.1 convolution_bitcast_fusion.15
  323.9 2.1 convolution_bitcast_fusion.15
  344.3 2.1 convolution_bitcast_fusion.15
  364.6 2.1 convolution_bitcast_fusion.15
  385.0 2.1 convolution_bitcast_fusion.15
  397.7 2.8 broadcast_multiply_fusion
  400.5 70.0 %reduce-scatter.2.cloned.1.call-done = f32[32,2,2,512]{3,0,2,1:T(8,128)} async-done(((f32[512,2,2,512]{3,0,2,1:T(8,128)}), f32[32,2,2,512]{3,0,2,1:T(8,128)}) %reduce-scatter.2.cloned.1.call-update) | async-done | bytes 262160 | tf_op jit(solution)/shard_map/reduce_scatter | solution.py:164
  472.2 3.4 all-to-all-start.1
  477.8 7.3 %reshape.109 = bf16[2,256,4096]{2,1,0:T(8,128)(2,1)} reshape(bf16[2,256,4,8,128]{4,3,2,1,0:T(8,128)(2,1)} %get-tuple-element.274) | data formatting | bytes 8388608 | tf_op jit(solution)/shard_map/reshape | solution.py:156
  485.1 7.3 %reshape.110 = bf16[2,256,4096]{2,1,0:T(8,128)(2,1)} reshape(bf16[2,256,4,8,128]{4,3,2,1,0:T(8,128)(2,1)} %get-tuple-element.275) | data formatting | bytes 8388608 | tf_op jit(solution)/shard_map/reshape | solution.py:157
  (688 shorter events, 302.7 us)
Async XLA Ops:
  7.2 11.9 %copy-start.3 = (bf16[2,256,2,512]{3,2,1,0:T(2,128)(2,1)S(1)}, bf16[2,256,2,512]{3,2,1,0:T(2,128)(2,1)}, u32[]{:S(2)}) copy-start(bf16[2,256,2,512]{3,2,1,0:T(2,128)(2,1)} %param.10) | copy-start | bytes 3145732
  7.2 52.2 %all-gather.2.cloned.1.call-start = ((), (), s32[]{:S(2)}) async-start(), calls=%async_computation.3 | async-start | bytes 2228224 | tf_op jit(solution)/shard_map/all_gather | solution.py:47
  15.6 454.9 %reduce-scatter.2.cloned.1.call-start = ((), (), s32[]{:S(2)}) async-start(), calls=%async_computation.4 | async-start | bytes 4456448 | tf_op jit(solution)/shard_map/reduce_scatter | solution.py:164
  27.6 7.6 %copy-start.4 = (s32[2]{0:T(128)S(1)}, s32[2]{0:T(128)}, u32[]{:S(2)}) copy-start(s32[2]{0:T(128)} %param.15) | copy-start | bytes 28
  85.3 1.0 copy-start.2
  86.2 1.3 copy-start
  105.6 1.0 copy-start.2
  106.6 1.3 copy-start
  126.0 1.0 copy-start.2
  126.9 1.3 copy-start
  147.3 1.3 copy-start
  166.7 1.0 copy-start.2
  167.7 1.3 copy-start
  187.0 1.0 copy-start.2
  188.0 1.3 copy-start
  207.4 1.0 copy-start.2
  208.3 1.3 copy-start
  227.7 1.0 copy-start.2
  228.6 1.3 copy-start
  248.0 1.0 copy-start.2
  249.0 1.3 copy-start
  268.4 1.0 copy-start.2
  269.3 1.3 copy-start
  288.7 1.0 copy-start.2
  289.6 1.3 copy-start
  310.0 1.3 copy-start
  330.3 1.3 copy-start
  350.7 1.3 copy-start
  371.0 1.3 copy-start
  391.4 1.3 copy-start
  400.4 75.1 %copy-start.1 = (f32[2,256,2,4,128]{4,1,0,2,3:T(8,128)S(1)}, f32[2,256,2,4,128]{4,1,0,2,3:T(8,128)}, u32[]{:S(2)}) copy-start(f32[2,256,2,4,128]{4,1,0,2,3:T(8,128)} %get-tuple-element.276) | copy-start | bytes 6291460
  472.2 20.2 %all-to-all-start.1 = ((bf16[2,16,2,2,4,128]{5,4,1,3,2,0:T(4,128)(2,1)}), bf16[2,16,2,2,4,128]{5,4,1,3,2,0:T(4,128)(2,1)S(1)}, u32[]{:S(2)}, u32[]{:S(2)}) async-start(bf16[2,16,2,2,4,128]{5,4,1,3,2,0:T(4,128)(2,1)} %copy.170), calls=%async_computation.2 | async-start | bytes 262144 | tf_op jit(solution)/shard_map/all_to_all | solution.py:170
  (6 other events, 5.7 us)
Sparse Core Ops, SparseCore 0:
  15.7 43.6 all-gather.1
  400.6 69.8 reduce-scatter.1
where the time goes:
time: 507 us; the launch traced here: 500 us
  local copies, waits for them, and re-layouts  201 us (40%)
  matrix products  118 us (23%)
  waiting for transfers between devices  89.7 us (18%)
  other arithmetic  62.2 us (12%)
  between operations  16.1 us (3%)
  blocking collectives  6.43 us (1%)
    reduce_scatter x1, waiting for transfers between devices, on_device(): lax.psum_scatter(picked[:, None] * mine_float[None, :, None, None], 'dp',...  70 us
    dot_general x16, matrix products, attend(): jnp.einsum('resj,rseh->jh', far_b, grad_block, preferred_element_type=jnp...  33.3 us
    dynamic_update_slice x16, other arithmetic, attend(): lax.dynamic_update_slice(own_grad, own_now + jnp.stack([near_dk, near_dv]...  30.5 us
    dynamic_update_slice x32, local copies, waits for them, and re-layouts, attend(): dq_buf = lax.dynamic_update_slice(dq_buf, grad_query[:, :, None], corner)  21 us
    dynamic_slice x32, local copies, waits for them, and re-layouts, attend(): lax.dynamic_slice(prefix_grad, prefix_corner, (PROMPT_LENGTH, 2, 1, head_...  20.4 us
    all_gather x1, waiting for transfers between devices, on_device(): lax.all_gather(regrouped, 'dp', axis=0, tiled=True)  19.7 us
    dynamic_slice x32, local copies, waits for them, and re-layouts, attend(): grad_block = lax.dynamic_slice(active_gradient, corner, extent)[:, :, 0]  18.4 us
    dynamic_slice x32, local copies, waits for them, and re-layouts, attend(): own_kv = lax.dynamic_index_in_dim(own_all, kv_head, 3, keepdims=False)  18.4 us
  transfers between devices with their start and end apart: 3, of which 2 were waited for; matrix products, arithmetic and copies ran while one was open for 8% of the time, Pallas kernels for 0%

commit v1 on v0

v1 whole, which is shorter than its diff:
```python
import functools
import math

import jax
import jax.numpy as jnp
from jax import lax
from jax.experimental import pallas as pl
from jax.experimental.pallas import tpu as pltpu
from jax.sharding import PartitionSpec as P

HEAD = 128
F32 = jnp.float32
BF16 = jnp.bfloat16
SCALE = HEAD ** (-0.5)
LOG2_SCALE = SCALE * math.log2(math.e)
NT = ((1,), (1,))
NN = ((1,), (0,))
TN = ((0,), (0,))


def dot(a, b, dims):
    return lax.dot_general(a, b, (dims, ((), ())), preferred_element_type=F32)


def attention_kernel(
    tile_rows,
    head_block,
    group,
    len_ref,
    query_ref,
    grad_ref,
    far_key_ref,
    far_value_ref,
    own_key_ref,
    own_value_ref,
    out_ref,
    dquery_ref,
    own_dkey_ref,
    own_dvalue_ref,
    far_dkey_ref,
    far_dvalue_ref,
    far_dk,
    far_dv,
    own_dk,
    own_dv,
):
    response = pl.program_id(1)
    live_count = len_ref[response]
    row_count = query_ref.shape[1]
    tall = head_block * tile_rows

    @pl.when(response == 0)
    def _():
        far_dk[...] = jnp.zeros_like(far_dk)
        far_dv[...] = jnp.zeros_like(far_dv)

    own_dk[...] = jnp.zeros_like(own_dk)
    own_dv[...] = jnp.zeros_like(own_dv)

    def tile(first_row, first_head):
        columns = [
            pl.ds(pl.multiple_of((first_head + j) * HEAD, HEAD), HEAD) for j in range(head_block)
        ]
        rows = pl.ds(first_row, tile_rows)
        near_count = first_row + tile_rows
        query = jnp.concatenate([query_ref[0, rows, c] for c in columns], 0)
        grad = jnp.concatenate([grad_ref[0, rows, c] for c in columns], 0)
        far_key = far_key_ref[...]
        far_value = far_value_ref[...]
        own_key = own_key_ref[0, pl.ds(0, near_count), :]
        own_value = own_value_ref[0, pl.ds(0, near_count), :]
        row_in_tile = lax.broadcasted_iota(jnp.int32, (tall, 1), 0) % tile_rows
        live = row_in_tile + first_row < live_count
        far_score = dot(query, far_key, NT)
        near_score = dot(query, own_key, NT)
        row = lax.broadcasted_iota(jnp.int32, (tall, tile_rows), 0) % tile_rows
        column = lax.broadcasted_iota(jnp.int32, (tall, tile_rows), 1)
        corner = jnp.where(column <= row, near_score[:, first_row:], -jnp.inf)
        near_score = jnp.concatenate([near_score[:, :first_row], corner], 1) if first_row else corner
        peak = jnp.maximum(
            jnp.max(far_score, 1, keepdims=True), jnp.max(near_score, 1, keepdims=True)
        )
        far_exp = jnp.exp2((far_score - peak) * LOG2_SCALE)
        near_exp = jnp.exp2((near_score - peak) * LOG2_SCALE)
        total = jnp.sum(far_exp, 1, keepdims=True) + jnp.sum(near_exp, 1, keepdims=True)
        inverse = jnp.where(live, 1.0 / total, 0.0)
        far_b = far_exp.astype(BF16)
        near_b = near_exp.astype(BF16)
        out = ((dot(far_b, far_value, NN) + dot(near_b, own_value, NN)) * inverse).astype(BF16)
        grad = (grad.astype(F32) * inverse).astype(BF16)
        delta = jnp.sum(grad.astype(F32) * out.astype(F32), 1, keepdims=True)
        far_ds = (far_exp * (dot(grad, far_value, NT) - delta)).astype(BF16)
        near_ds = (near_exp * (dot(grad, own_value, NT) - delta)).astype(BF16)
        dquery = ((dot(far_ds, far_key, NN) + dot(near_ds, own_key, NN)) * SCALE).astype(BF16)
        for j, c in enumerate(columns):
            out_ref[0, rows, c] = out[j * tile_rows : (j + 1) * tile_rows]
            dquery_ref[0, rows, c] = dquery[j * tile_rows : (j + 1) * tile_rows]
        far_dk[...] += dot(query, far_ds, TN)
        far_dv[...] += dot(grad, far_b, TN)
        own_dk[:, :near_count] += dot(query, near_ds, TN)
        own_dv[:, :near_count] += dot(grad, near_b, TN)

    for first_row in range(0, row_count, tile_rows):

        @pl.when(first_row < live_count)
        def _(first_row=first_row):
            def step(i, carry):
                tile(first_row, i * head_block)
                return carry

            lax.fori_loop(0, group // head_block, step, 0)

        if first_row:

            @pl.when(first_row >= live_count)
            def _(first_row=first_row):
                blank = jnp.zeros((tile_rows, group * HEAD), BF16)
                out_ref[0, pl.ds(first_row, tile_rows), :] = blank
                dquery_ref[0, pl.ds(first_row, tile_rows), :] = blank

    own_dkey_ref[0] = (own_dk[...].T * SCALE).astype(BF16)
    own_dvalue_ref[0] = own_dv[...].T.astype(BF16)

    @pl.when(response == pl.num_programs(1) - 1)
    def _():
        far_dkey_ref[...] = (far_dk[...].T * SCALE).astype(BF16)
        far_dvalue_ref[...] = far_dv[...].T.astype(BF16)


def attention_grads(queries, grad_out, own_kv, prefix, resp_len):
    responses, rows, width = queries.shape
    kv_local = own_kv.shape[2] // (2 * HEAD)
    group = width // HEAD // kv_local
    prompt_rows = prefix.shape[0]
    tile_rows = 128
    head_block = math.gcd(group, 4)
    wide = pl.BlockSpec((1, rows, group * HEAD), lambda a, r, *_: (r, 0, a))
    own_k = pl.BlockSpec((1, rows, HEAD), lambda a, r, *_: (r, 0, a))
    own_v = pl.BlockSpec((1, rows, HEAD), lambda a, r, *_: (r, 0, kv_local + a))
    far_k = pl.BlockSpec((prompt_rows, HEAD), lambda a, r, *_: (0, a))
    far_v = pl.BlockSpec((prompt_rows, HEAD), lambda a, r, *_: (0, kv_local + a))
    own_shape = jax.ShapeDtypeStruct((responses, rows, kv_local * HEAD), BF16)
    far_shape = jax.ShapeDtypeStruct((prompt_rows, kv_local * HEAD), BF16)
    return pl.pallas_call(
        functools.partial(attention_kernel, tile_rows, head_block, group),
        grid_spec=pltpu.PrefetchScalarGridSpec(
            num_scalar_prefetch=1,
            grid=(kv_local, responses),
            in_specs=[wide, wide, far_k, far_v, own_k, own_v],
            out_specs=[wide, wide, own_k, own_k, far_k, far_k],
            scratch_shapes=[
                pltpu.VMEM((HEAD, prompt_rows), F32),
                pltpu.VMEM((HEAD, prompt_rows), F32),
                pltpu.VMEM((HEAD, rows), F32),
                pltpu.VMEM((HEAD, rows), F32),
            ],
        ),
        out_shape=[
            jax.ShapeDtypeStruct(queries.shape, BF16),
            jax.ShapeDtypeStruct(queries.shape, BF16),
            own_shape,
            own_shape,
            far_shape,
            far_shape,
        ],
        compiler_params=pltpu.CompilerParams(vmem_limit_bytes=48 << 20),
        name="attention_grads",
    )(resp_len, queries, grad_out, prefix, prefix, own_kv, own_kv)


def on_device(queries, resp_kv, prefix_pool, grad_out, member_list, prompt_slot, resp_len):
    dp_count = lax.axis_size("dp")
    tensor_count = lax.axis_size("tensor")
    responses, rows = queries.shape[:2]
    kv_width = resp_kv.shape[3]
    slice_rows, slot_count = prefix_pool.shape[:2]
    prompt_count = member_list.shape[0]
    everyone = ("dp", "tensor")

    owner_hit = member_list[:, :, None] == jnp.arange(dp_count, dtype=jnp.int32)[None, None, :]
    slot_of = jnp.sum(jnp.where(owner_hit, prompt_slot[:, None, None], 0), axis=(0, 1))

    pool = prefix_pool.reshape(slice_rows, slot_count, 2, tensor_count, kv_width)
    wanted = slot_of[:, None, None, None, None]
    outgoing = jnp.zeros((), BF16)
    for slot in range(slot_count):
        part = pool[:, slot].transpose(2, 0, 1, 3)[None]
        outgoing = part if slot == 0 else jnp.where(wanted == slot, part, outgoing)
    outgoing = outgoing.reshape(dp_count * tensor_count, slice_rows, 2 * kv_width)
    prefix = lax.all_to_all(outgoing, everyone, split_axis=0, concat_axis=0, tiled=True)
    prefix = prefix.reshape(dp_count * tensor_count * slice_rows, 2 * kv_width)

    own_kv = resp_kv.reshape(responses, rows, 2 * kv_width)
    attention, grad_queries, own_dk, own_dv, far_dk, far_dv = attention_grads(
        queries, grad_out, own_kv, prefix, resp_len
    )
    grad_resp_kv = jnp.stack([own_dk, own_dv], axis=2)

    partial = jnp.stack([far_dk, far_dv], axis=1)
    partial = partial.reshape(dp_count * tensor_count, slice_rows, 2 * kv_width)
    arrived = lax.all_to_all(partial, everyone, split_axis=0, concat_axis=0, tiled=True)
    arrived = arrived.reshape(dp_count, tensor_count, slice_rows, 2, kv_width).astype(F32)
    sums = []
    for slot in range(slot_count):
        sums.append(jnp.sum(jnp.where(wanted == slot, arrived, 0.0), axis=0))
    grad_prefix = jnp.stack(sums, 0).transpose(2, 0, 3, 1, 4).astype(BF16)
    grad_prefix = grad_prefix.reshape(slice_rows, slot_count, 2, tensor_count * kv_width)
    return attention, grad_queries, grad_resp_kv, grad_prefix


def solution(mesh):
    return jax.shard_map(
        on_device,
        mesh=mesh,
        in_specs=(
            P("dp", None, "tensor"),
            P("dp", None, None, "tensor"),
            P(("dp", "tensor"), None, None, None),
            P("dp", None, "tensor"),
            P(),
            P(),
            P("dp"),
        ),
        out_specs=(
            P("dp", None, "tensor"),
            P("dp", None, "tensor"),
            P("dp", None, None, "tensor"),
            P(("dp", "tensor"), None, None, None),
        ),
        check_vma=False,
    )
```

time: 507 us -> 134 us (0.26); the launches traced: 500 us -> 133 us
  local copies, waits for them, and re-layouts: 201 us -> 14.2 us
  matrix products: 118 us -> 0 us
  other arithmetic: 62.2 us -> 4.47 us
  Pallas kernels: 0 us -> 53.9 us
  waiting for transfers between devices: 89.7 us -> 49.1 us
  between operations: 16.1 us -> 0.78 us
  starting transfers between devices: 3.46 us -> 11 us
  blocking collectives: 6.43 us -> 0 us
    dot_general x192 -> x0, matrix products: 118 us -> none  [the longest x16 33.3 us: attend(): jnp.einsum('resj,rseh->jh', far_b, grad_block, preferred_element_type=jnp...]
    dynamic_slice x131 -> x0, local copies, waits for them, and re-layouts: 78.7 us -> none  [the longest x32 20.4 us: attend(): lax.dynamic_slice(prefix_grad, prefix_corner, (PROMPT_LENGTH, 2, 1, head_...]
    reduce_scatter x1 -> x0, waiting for transfers between devices: 70 us -> none  [on_device(): lax.psum_scatter(picked[:, None] * mine_float[None, :, None, None], 'dp',...]
    dynamic_update_slice x80 -> x0, local copies, waits for them, and re-layouts: 55.5 us -> none  [the longest x32 21 us: attend(): dq_buf = lax.dynamic_update_slice(dq_buf, grad_query[:, :, None], corner)]
    pallas_call x0 -> x1, Pallas kernels: none -> 53.9 us  [attention_grads(): pl.pallas_call(functools.partial(attention_kernel, tile_rows, head_block,...]
    all_to_all x1 -> x2, waiting for transfers between devices: 0.01 us -> 49.1 us  [the longest x1 25.2 us: on_device(): lax.all_to_all(outgoing, everyone, split_axis=0, concat_axis=0, tiled=True)]
    dynamic_update_slice x16 -> x0, other arithmetic: 30.5 us -> none  [attend(): lax.dynamic_update_slice(own_grad, own_now + jnp.stack([near_dk, near_dv]...]
    all_gather x1 -> x0, waiting for transfers between devices: 19.7 us -> none  [on_device(): lax.all_gather(regrouped, 'dp', axis=0, tiled=True)]
  transfers between devices with their start and end apart: 3 -> 2, of which waited for: 2 -> 2; matrix products, arithmetic and copies ran while one was open for 8% -> 2% of each run, Pallas kernels for 0% -> 0%
where the time goes in v1:
time: 134 us; the launch traced here: 133 us
  Pallas kernels  53.9 us (40%)
  waiting for transfers between devices  49.1 us (37%)
  local copies, waits for them, and re-layouts  14.2 us (11%)
  starting transfers between devices  11 us (8%)
  other arithmetic  4.47 us (3%)
    pallas_call x1, Pallas kernels, attention_grads(): pl.pallas_call(functools.partial(attention_kernel, tile_rows, head_block,...  53.9 us
    all_to_all x1, waiting for transfers between devices, on_device(): lax.all_to_all(outgoing, everyone, split_axis=0, concat_axis=0, tiled=True)  25.2 us
    all_to_all x1, waiting for transfers between devices, on_device(): lax.all_to_all(partial, everyone, split_axis=0, concat_axis=0, tiled=True)  23.9 us
    all_to_all x1, starting transfers between devices, on_device(): lax.all_to_all(outgoing, everyone, split_axis=0, concat_axis=0, tiled=True)  7.1 us
    all_to_all x1, starting transfers between devices, on_device(): lax.all_to_all(partial, everyone, split_axis=0, concat_axis=0, tiled=True)  3.92 us
    broadcast_in_dim x6, local copies, waits for them, and re-layouts, on_device(): outgoing = part if slot == 0 else jnp.where(wanted == slot, part, outgoing)  3.57 us
    convert_element_type x1, local copies, waits for them, and re-layouts, on_device(): arrived.reshape(dp_count, tensor_count, slice_rows, 2, kv_width).astype(F32)  3.12 us
    unnamed x7, local copies, waits for them, and re-layouts  2.94 us
  transfers between devices with their start and end apart: 2, of which 2 were waited for; matrix products, arithmetic and copies ran while one was open for 2% of the time, Pallas kernels for 0%

profile of v1, /device:TPU:1, one launch (start us, length us, event | category | flops | bytes accessed | tf_op | source)
XLA Modules:
  0.0 133.5 jit_solution(8705117429149768756)
XLA Ops:
  0.6 0.8 select_reduce_fusion.2
  1.4 0.1 broadcast_in_dim.70
  1.5 0.1 broadcast_in_dim.71
  1.6 1.0 reshape.42
  2.6 0.1 slice_bitcast_fusion
  2.7 0.1 copy.29
  2.8 0.1 copy.28
  2.8 0.9 broadcast_in_dim.73
  3.8 0.8 broadcast_in_dim.74
  4.5 0.9 broadcast_in_dim.75
  5.5 0.8 broadcast_in_dim.76
  6.3 0.0 copy-start.1
  6.3 1.1 broadcast_select_fusion
  7.4 0.0 copy-start
  7.4 7.1 %all-to-all-start = ((bf16[32,16,1024]{2,1,0:T(8,128)(2,1)}), bf16[32,16,1024]{2,1,0:T(8,128)(2,1)S(1)}, u32[]{:S(2)}, u32[]{:S(2)}) async-start(bf16[32,16,1024]{2,1,0:T(8,128)(2,1)} %broadcast_select_fusion), calls=%async_computation | async-start | bytes 2097152 | tf_op jit(solution)/shard_map/all_to_all | solution.py:190
  14.5 0.0 copy-done.1
  14.5 0.8 reshape.44.own_key_ref.own_value_ref
  15.3 25.2 %all-to-all-done = bf16[32,16,1024]{2,1,0:T(8,128)(2,1)S(1)} async-done(((bf16[32,16,1024]{2,1,0:T(8,128)(2,1)}), bf16[32,16,1024]{2,1,0:T(8,128)(2,1)S(1)}, u32[]{:S(2)}, u32[]{:S(2)}) %all-to-all-start) | async-done | bytes 1048608 | tf_op jit(solution)/shard_map/all_to_all | solution.py:190
  40.5 0.0 copy-done
  40.5 53.9 %attention_grads.1 = (bf16[2,256,4096]{2,1,0:T(8,128)(2,1)}, bf16[2,256,4096]{2,1,0:T(8,128)(2,1)}, bf16[2,256,512]{2,1,0:T(8,128)(2,1)S(1)}, bf16[2,256,512]{2,...) custom-call(s32[2]{0:T(128)S(1)} %copy-done, bf16[2,256,4096]{2,1,0:T(8,128)(2,1)} %query_ref.1, ...), custom_call_target="tpu_custom_call" | custom-call | tf_op jit(solution)/shard_map/attention_grads/pallas_call | solution.py:144
  94.4 0.1 pad_maximum_fusion.1
  94.5 1.1 copy.30
  95.6 1.6 %reshape.45 = bf16[32,16,1024]{2,1,0:T(8,128)(2,1)} reshape(bf16[512,2,512]{2,1,0:T(2,128)(2,1)S(1)} %copy.30) | data formatting | bytes 2097152 | tf_op jit(solution)/shard_map/reshape | solution.py:200
  97.1 3.9 %all-to-all-start.1 = ((bf16[32,16,1024]{2,1,0:T(8,128)(2,1)}), bf16[32,16,1024]{2,1,0:T(8,128)(2,1)}, u32[]{:S(2)}, u32[]{:S(2)}) async-start(bf16[32,16,1024]{2,1,0:T(8,128)(2,1)} %reshape.45), calls=%async_computation.1 | async-start | bytes 2097152 | tf_op jit(solution)/shard_map/all_to_all | solution.py:201
  101.1 0.1 pad_maximum_fusion
  101.2 2.0 %copy.32 = bf16[2,256,2,512]{3,2,1,0:T(2,128)(2,1)} copy(bf16[2,256,2,512]{3,1,0,2:T(8,128)(2,1)S(1)} %pad_maximum_fusion) | data formatting | bytes 2097152
  103.2 23.9 %all-to-all-done.1 = bf16[32,16,1024]{2,1,0:T(8,128)(2,1)} async-done(((bf16[32,16,1024]{2,1,0:T(8,128)(2,1)}), bf16[32,16,1024]{2,1,0:T(8,128)(2,1)}, u32[]{:S(2)}, u32[]{:S(2)}) %all-to-all-start.1) | async-done | bytes 1048608 | tf_op jit(solution)/shard_map/all_to_all | solution.py:201
  127.1 3.1 %reshape.47 = f32[16,2,16,2,512]{4,3,2,1,0:T(2,128)S(1)} reshape(bf16[32,16,1024]{2,1,0:T(8,128)(2,1)} %all-to-all-done.1) | data formatting | bytes 3145728 | tf_op jit(solution)/shard_map/convert_element_type | solution.py:202
  130.2 2.2 %select_reduce_fusion.1 = (bf16[2,16,2,512]{3,2,1,0:T(2,128)(2,1)S(1)}, bf16[2,16,2,512]{3,2,1,0:T(2,128)(2,1)S(1)}) fusion(f32[16,2,16,2,512]{4,3,2,1,0:T(2,128)S(1)} %reshape.47, pred[16]{0:T(512)(128)(4,1)S(1)} %get-tuple-element.40, pred[16]{0:T(512)(128)(4,1)S(1)} %get-tuple-element.41), kind=kLoop, calls=%fused_computation.1 | loop fusion | flops 2031616 | bytes 2228256 | tf_op jit(solution)/shard_map/reduce_sum | solution.py:205
  132.4 0.2 maximum_bitcast_fusion
  132.6 0.1 copy.34
  132.7 0.7 reshape.48
  (1 shorter events, 0.0 us)
Async XLA Ops:
  6.3 8.3 %copy-start.1 = (bf16[2,256,2,512]{3,2,1,0:T(2,128)(2,1)S(1)}, bf16[2,256,2,512]{3,2,1,0:T(2,128)(2,1)}, u32[]{:S(2)}) copy-start(bf16[2,256,2,512]{3,2,1,0:T(2,128)(2,1)} %param.8) | copy-start | bytes 3145732
  7.4 33.1 %copy-start = (s32[2]{0:T(128)S(1)}, s32[2]{0:T(128)}, u32[]{:S(2)}) copy-start(s32[2]{0:T(128)} %len_ref.1) | copy-start | bytes 28
  7.4 33.1 %all-to-all-start = ((bf16[32,16,1024]{2,1,0:T(8,128)(2,1)}), bf16[32,16,1024]{2,1,0:T(8,128)(2,1)S(1)}, u32[]{:S(2)}, u32[]{:S(2)}) async-start(bf16[32,16,1024]{2,1,0:T(8,128)(2,1)} %broadcast_select_fusion), calls=%async_computation | async-start | bytes 2097152 | tf_op jit(solution)/shard_map/all_to_all | solution.py:190
  97.1 30.0 %all-to-all-start.1 = ((bf16[32,16,1024]{2,1,0:T(8,128)(2,1)}), bf16[32,16,1024]{2,1,0:T(8,128)(2,1)}, u32[]{:S(2)}, u32[]{:S(2)}) async-start(bf16[32,16,1024]{2,1,0:T(8,128)(2,1)} %reshape.45), calls=%async_computation.1 | async-start | bytes 2097152 | tf_op jit(solution)/shard_map/all_to_all | solution.py:201

commit v2 on v1

v2 whole, which is shorter than its diff:
```python
import functools
import math

import jax
import jax.numpy as jnp
from jax import lax
from jax.experimental import pallas as pl
from jax.experimental.pallas import tpu as pltpu
from jax.sharding import PartitionSpec as P

HEAD = 128
F32 = jnp.float32
BF16 = jnp.bfloat16
SCALE = HEAD ** (-0.5)
LOG2_SCALE = SCALE * math.log2(math.e)
NT = ((1,), (1,))
NN = ((1,), (0,))
TN = ((0,), (0,))
EVERYONE = ("dp", "tensor")
VMEM_LIMIT = 56 << 20


def dot(a, b, dims):
    return lax.dot_general(a, b, (dims, ((), ())), preferred_element_type=F32)


def attention_kernel(tile_rows, head_block, group, *refs):
    len_ref, query_ref, grad_ref, far_ref, own_key_ref, own_value_ref = refs[:6]
    out_ref, dquery_ref, own_dkey_ref, own_dvalue_ref, far_grad_ref = refs[-9:-4]
    keys, values, dkeys, dvalues = refs[-4:]
    response = pl.program_id(1)
    live_count = len_ref[response]
    row_count = query_ref.shape[1]
    prompt_rows = far_ref.shape[0]
    tall = head_block * tile_rows
    far_rows = pl.ds(0, prompt_rows)
    own_rows = pl.ds(prompt_rows, row_count)

    def hold(rows, key, value):
        keys[rows, :HEAD] = key
        keys[rows, HEAD:] = key
        values[rows, :] = value

    @pl.when(response == 0)
    def _():
        hold(far_rows, far_ref[:, :HEAD], far_ref[:, HEAD:])
        dkeys[:, :prompt_rows] = jnp.zeros((HEAD, prompt_rows), F32)
        dvalues[:, :prompt_rows] = jnp.zeros((HEAD, prompt_rows), F32)

    hold(own_rows, own_key_ref[0], own_value_ref[0])
    dkeys[:, prompt_rows:] = jnp.zeros((HEAD, row_count), F32)
    dvalues[:, prompt_rows:] = jnp.zeros((HEAD, row_count), F32)

    def score(c):
        c["query"] = jnp.concatenate([query_ref[0, c["rows"], s] for s in c["columns"]], 0)
        scaled = c["query"].astype(F32) * LOG2_SCALE
        high = scaled.astype(BF16)
        low = (scaled - high.astype(F32)).astype(BF16)
        c["score"] = dot(jnp.concatenate([high, low], 1), keys[: c["count"]], NT)

    def softmax(c):
        scores, count = c.pop("score"), c["count"]
        row = lax.broadcasted_iota(jnp.int32, (tall, tile_rows), 0) % tile_rows
        column = lax.broadcasted_iota(jnp.int32, (tall, tile_rows), 1)
        corner = jnp.where(column <= row, scores[:, count - tile_rows :], -jnp.inf)
        scores = jnp.concatenate([scores[:, : count - tile_rows], corner], 1)
        exps = jnp.exp2(scores - jnp.max(scores, 1, keepdims=True))
        c["exps"] = exps.astype(BF16)
        place = lax.broadcasted_iota(jnp.int32, (tall, 1), 0) % tile_rows + c["first_row"]
        c["inverse"] = jnp.where(
            place < live_count, 1.0 / jnp.sum(exps, 1, keepdims=True), 0.0
        )

    def attend(c):
        inverse, value = c.pop("inverse"), values[: c["count"]]
        out = (dot(c["exps"], value, NN) * inverse).astype(BF16)
        grad = jnp.concatenate([grad_ref[0, c["rows"], s] for s in c["columns"]], 0)
        c["grad"] = grad = (grad.astype(F32) * inverse).astype(BF16)
        c["delta"] = jnp.sum(grad.astype(F32) * out.astype(F32), 1, keepdims=True)
        for j, s in enumerate(c["columns"]):
            out_ref[0, c["rows"], s] = out[j * tile_rows : (j + 1) * tile_rows]
        c["dprobs"] = dot(grad, value, NT)

    def dscore(c):
        c["dscore"] = c["exps"] * (c.pop("dprobs") - c.pop("delta")).astype(BF16)

    def dquery(c):
        result = (dot(c["dscore"], keys[: c["count"], :HEAD], NN) * SCALE).astype(BF16)
        for j, s in enumerate(c["columns"]):
            dquery_ref[0, c["rows"], s] = result[j * tile_rows : (j + 1) * tile_rows]

    def dkey_dvalue(c):
        dkeys[:, : c["count"]] += dot(c["query"], c["dscore"], TN)
        dvalues[:, : c["count"]] += dot(c["grad"], c["exps"], TN)

    stages = (score, softmax, attend, dscore, dquery, dkey_dvalue)

    def work(tiles):
        chains = [
            {
                "columns": [pl.ds((h + j) * HEAD, HEAD) for j in range(head_block)],
                "rows": pl.ds(t, tile_rows),
                "first_row": t,
                "count": prompt_rows + t + tile_rows,
            }
            for h in range(0, group, head_block)
            for t in tiles
        ]
        for step in range(len(stages) + len(chains) - 1):
            for i, chain in enumerate(chains):
                if 0 <= step - i < len(stages):
                    stages[step - i](chain)

    starts = list(range(0, row_count, tile_rows))
    for k in range(len(starts)):
        last = k + 1 == len(starts)
        upper = row_count if last else starts[k + 1]

        @pl.when((live_count > starts[k]) & (last | (live_count <= upper)))
        def _(k=k, last=last, upper=upper):
            work(starts[: k + 1])
            if not last:
                blank = jnp.zeros((row_count - upper, group * HEAD), BF16)
                out_ref[0, upper:, :] = blank
                dquery_ref[0, upper:, :] = blank

    own_dkey_ref[0] = (dkeys[:, prompt_rows:].T * SCALE).astype(BF16)
    own_dvalue_ref[0] = dvalues[:, prompt_rows:].T.astype(BF16)

    @pl.when(response == pl.num_programs(1) - 1)
    def _():
        far_grad_ref[:, :HEAD] = (dkeys[:, :prompt_rows].T * SCALE).astype(BF16)
        far_grad_ref[:, HEAD:] = dvalues[:, :prompt_rows].T.astype(BF16)


def attention_grads(queries, grad_out, own_kv, prefix, resp_len, base, held):
    responses, rows, width = queries.shape
    kv_local = own_kv.shape[2] // (2 * HEAD)
    group = width // HEAD // kv_local
    prompt_rows = prefix.shape[0]
    heads = prefix.shape[1] // (2 * HEAD)
    tile_rows = min(128, rows)
    head_block = math.gcd(group, 4)
    wide = pl.BlockSpec((1, rows, group * HEAD), lambda a, r, *_: (r, 0, a + base))
    own_k = pl.BlockSpec((1, rows, HEAD), lambda a, r, *_: (r, 0, a + base))
    own_v = pl.BlockSpec((1, rows, HEAD), lambda a, r, *_: (r, 0, a + base + kv_local))
    far = pl.BlockSpec((prompt_rows, 2 * HEAD), lambda a, r, *_: (0, a))
    anywhere = pl.BlockSpec(memory_space=pl.ANY)
    own_shape = jax.ShapeDtypeStruct((responses, rows, kv_local * HEAD), BF16)
    pairs = responses * rows * group * heads * (prompt_rows + rows)
    return pl.pallas_call(
        functools.partial(attention_kernel, tile_rows, head_block, group),
        grid_spec=pltpu.PrefetchScalarGridSpec(
            num_scalar_prefetch=1,
            grid=(heads, responses),
            in_specs=[wide, wide, far, own_k, own_v] + [anywhere] * len(held),
            out_specs=[wide, wide, own_k, own_k, far],
            scratch_shapes=[
                pltpu.VMEM((prompt_rows + rows, 2 * HEAD), BF16),
                pltpu.VMEM((prompt_rows + rows, HEAD), BF16),
                pltpu.VMEM((HEAD, prompt_rows + rows), F32),
                pltpu.VMEM((HEAD, prompt_rows + rows), F32),
            ],
        ),
        out_shape=[
            jax.ShapeDtypeStruct(queries.shape, BF16),
            jax.ShapeDtypeStruct(queries.shape, BF16),
            own_shape,
            own_shape,
            jax.ShapeDtypeStruct(prefix.shape, BF16),
        ],
        input_output_aliases={6 + i: i for i in range(len(held))},
        compiler_params=pltpu.CompilerParams(vmem_limit_bytes=VMEM_LIMIT),
        cost_estimate=pl.CostEstimate(
            flops=12 * HEAD * pairs,
            transcendentals=pairs,
            bytes_accessed=8 * responses * rows * group * heads * HEAD,
        ),
        name="attention_grads",
    )(resp_len, queries, grad_out, prefix, own_kv, own_kv, *held)


def outgoing_kernel(shape, chunks, member_ref, slot_ref, pool_ref, *out_refs):
    tensor_count, kv_local = shape
    prompts, members = member_ref.shape
    kv_width = kv_local * HEAD
    half = tensor_count * kv_width

    def one(i, carry):
        prompt = i // members
        owner = member_ref[prompt, i % members]
        start = pl.multiple_of(slot_ref[prompt] * 2 * half, HEAD)
        for t in range(tensor_count):
            for (base, heads), out_ref in zip(chunks, out_refs):
                for h in range(heads):
                    for part in range(2):
                        source = part * half + t * kv_width + (base + h) * HEAD
                        out_ref[owner * tensor_count + t, :, pl.ds((2 * h + part) * HEAD, HEAD)] = (
                            pool_ref[:, pl.ds(pl.multiple_of(start + source, HEAD), HEAD)]
                        )
        return carry

    lax.fori_loop(0, prompts * members, one, 0)


def total_kernel(shape, chunks, member_ref, slot_ref, *refs):
    tensor_count, kv_local = shape
    in_refs, out_ref = refs[:-1], refs[-1]
    prompts, members = member_ref.shape
    kv_width = kv_local * HEAD
    half = tensor_count * kv_width

    def one(prompt, carry):
        start = pl.multiple_of(slot_ref[prompt] * 2 * half, HEAD)
        for (base, heads), in_ref in zip(chunks, in_refs):
            for t in range(tensor_count):
                total = in_ref[member_ref[prompt, 0] * tensor_count + t].astype(F32)
                for m in range(1, members):
                    total += in_ref[member_ref[prompt, m] * tensor_count + t].astype(F32)
                total = total.astype(BF16)
                for h in range(heads):
                    for part in range(2):
                        target = part * half + t * kv_width + (base + h) * HEAD
                        out_ref[:, pl.ds(pl.multiple_of(start + target, HEAD), HEAD)] = total[
                            :, (2 * h + part) * HEAD : (2 * h + part + 1) * HEAD
                        ]
        return carry

    lax.fori_loop(0, prompts, one, 0)


SMEM = pl.BlockSpec(memory_space=pltpu.SMEM)
VMEM = pl.BlockSpec(memory_space=pltpu.VMEM)


def on_device(queries, resp_kv, prefix_pool, grad_out, member_list, prompt_slot, resp_len):
    dp_count = lax.axis_size("dp")
    tensor_count = lax.axis_size("tensor")
    devices = dp_count * tensor_count
    responses, rows = queries.shape[:2]
    kv_width = resp_kv.shape[3]
    kv_local = kv_width // HEAD
    slice_rows, slot_count = prefix_pool.shape[:2]
    shape = (tensor_count, kv_local)
    first = (kv_local + 1) // 2
    chunks = [(0, first)] + ([(first, kv_local - first)] if first < kv_local else [])
    params = pltpu.CompilerParams(vmem_limit_bytes=VMEM_LIMIT)

    outgoing = pl.pallas_call(
        functools.partial(outgoing_kernel, shape, chunks),
        in_specs=[SMEM, SMEM, VMEM],
        out_specs=[VMEM] * len(chunks),
        out_shape=[
            jax.ShapeDtypeStruct((devices, slice_rows, 2 * HEAD * heads), BF16)
            for _, heads in chunks
        ],
        compiler_params=params,
        name="outgoing_rows",
    )(member_list, prompt_slot, prefix_pool.reshape(slice_rows, -1))
    prefixes = [
        lax.all_to_all(block, EVERYONE, split_axis=0, concat_axis=0, tiled=True)
        for block in outgoing
    ]

    own_kv = resp_kv.reshape(responses, rows, 2 * kv_width)
    held, arrived = [], []
    for (base, heads), prefix in zip(chunks, prefixes):
        prefix = prefix.reshape(devices * slice_rows, 2 * HEAD * heads)
        *held, far_grad = attention_grads(
            queries, grad_out, own_kv, prefix, resp_len, base, held
        )
        far_grad = far_grad.reshape(devices, slice_rows, 2 * HEAD * heads)
        arrived.append(
            lax.all_to_all(far_grad, EVERYONE, split_axis=0, concat_axis=0, tiled=True)
        )
    attention, grad_queries, own_dkey, own_dvalue = held
    grad_resp_kv = jnp.stack([own_dkey, own_dvalue], axis=2)

    grad_prefix = pl.pallas_call(
        functools.partial(total_kernel, shape, chunks),
        in_specs=[SMEM, SMEM] + [VMEM] * len(chunks),
        out_specs=VMEM,
        out_shape=jax.ShapeDtypeStruct((slice_rows, prefix_pool.size // slice_rows), BF16),
        compiler_params=params,
        name="prefix_totals",
    )(member_list, prompt_slot, *arrived)
    return attention, grad_queries, grad_resp_kv, grad_prefix.reshape(prefix_pool.shape)


def solution(mesh):
    return jax.shard_map(
        on_device,
        mesh=mesh,
        in_specs=(
            P("dp", None, "tensor"),
            P("dp", None, None, "tensor"),
            P(("dp", "tensor"), None, None, None),
            P("dp", None, "tensor"),
            P(),
            P(),
            P("dp"),
        ),
        out_specs=(
            P("dp", None, "tensor"),
            P("dp", None, "tensor"),
            P("dp", None, None, "tensor"),
            P(("dp", "tensor"), None, None, None),
        ),
        check_vma=False,
    )
```

time: 134 us -> 124 us (0.925)
  blocking collectives: 0 us -> 62.5 us
  waiting for transfers between devices: 49.1 us -> 12.5 us
  Pallas kernels: 53.9 us -> 31.6 us
  starting transfers between devices: 11 us -> 5.61 us
  local copies, waits for them, and re-layouts: 14.2 us -> 9.5 us
  other arithmetic: 4.47 us -> 1.3 us
    all_to_all x0 -> x2, blocking collectives: none -> 62.5 us  [the longest x1 39.4 us: on_device(): lax.all_to_all(far_grad, EVERYONE, split_axis=0, concat_axis=0, tiled=True)]
    all_to_all x2, waiting for transfers between devices: 49.1 us -> 12.5 us  [the longest x1 12.5 us: on_device(): lax.all_to_all(far_grad, EVERYONE, split_axis=0, concat_axis=0, tiled=True)]
    pallas_call x1 -> x2, Pallas kernels: 53.9 us -> 27.2 us  [attention_grads(): pl.pallas_call(functools.partial(attention_kernel, tile_rows, head_block,...]
    all_to_all x2, starting transfers between devices: 11 us -> 5.61 us  [the longest x1 2.8 us: on_device(): lax.all_to_all(block, EVERYONE, split_axis=0, concat_axis=0, tiled=True)]
    pallas_call x0 -> x2, Pallas kernels: none -> 4.39 us  [the longest x1 2.37 us: on_device(): pl.pallas_call(functools.partial(outgoing_kernel, shape, chunks), in_spec...]
    broadcast_in_dim x6 -> x0, local copies, waits for them, and re-layouts: 3.57 us -> none  [on_device(): outgoing = part if slot == 0 else jnp.where(wanted == slot, part, outgoing)]
    convert_element_type x1 -> x0, local copies, waits for them, and re-layouts: 3.12 us -> none  [on_device(): arrived.reshape(dp_count, tensor_count, slice_rows, 2, kv_width).astype(F32)]
    reduce_sum x2 -> x0, other arithmetic: 2.94 us -> none  [the longest x1 2.16 us: on_device(): sums.append(jnp.sum(jnp.where(wanted == slot, arrived, 0.0), axis=0))]
  transfers between devices with their start and end apart: 2 -> 2, of which waited for: 2 -> 1; matrix products, arithmetic and copies ran while one was open for 2% -> 5% of each run, Pallas kernels for 0% -> 11%
where the time goes in v2:
time: 124 us
  blocking collectives  62.5 us (50%)
  Pallas kernels  31.6 us (25%)
  waiting for transfers between devices  12.5 us (10%)
  local copies, waits for them, and re-layouts  9.5 us (8%)
  starting transfers between devices  5.61 us (5%)
  other arithmetic  1.3 us (1%)
    all_to_all x1, blocking collectives, on_device(): lax.all_to_all(far_grad, EVERYONE, split_axis=0, concat_axis=0, tiled=True)  39.4 us
    pallas_call x2, Pallas kernels, attention_grads(): pl.pallas_call(functools.partial(attention_kernel, tile_rows, head_block,...  27.2 us
    all_to_all x1, blocking collectives, on_device(): lax.all_to_all(block, EVERYONE, split_axis=0, concat_axis=0, tiled=True)  23 us
    all_to_all x1, waiting for transfers between devices, on_device(): lax.all_to_all(far_grad, EVERYONE, split_axis=0, concat_axis=0, tiled=True)  12.5 us
    unnamed x5, local copies, waits for them, and re-layouts  3.66 us
    all_to_all x1, starting transfers between devices, on_device(): lax.all_to_all(block, EVERYONE, split_axis=0, concat_axis=0, tiled=True)  2.8 us
    all_to_all x1, starting transfers between devices, on_device(): lax.all_to_all(far_grad, EVERYONE, split_axis=0, concat_axis=0, tiled=True)  2.8 us
    reshape x1, local copies, waits for them, and re-layouts, on_device(): own_kv = resp_kv.reshape(responses, rows, 2 * kv_width)  2.57 us
  transfers between devices with their start and end apart: 2, of which 1 were waited for; matrix products, arithmetic and copies ran while one was open for 5% of the time, Pallas kernels for 11%

profile of v2, /device:TPU:1, one launch (start us, length us, event | category | flops | bytes accessed | tf_op | source)
XLA Modules:
  0.0 123.6 jit_solution(16888069783020810942)
XLA Ops:
  0.6 1.6 %reshape.29.pool_ref = bf16[16,4096]{1,0:T(8,128)(2,1)} reshape(bf16[16,2,2,1024]{3,2,1,0:T(2,128)(2,1)} %param.9) | data formatting | bytes 262144 | tf_op jit(solution)/shard_map/reshape | solution.py:259
  2.3 2.4 %outgoing_rows.1 = (bf16[32,16,512]{2,1,0:T(8,128)(2,1)}, bf16[32,16,512]{2,1,0:T(8,128)(2,1)}) custom-call(s32[2,8]{1,0:T(2,128)} %member_ref.3, s32[2]{0:T(128)} %slot_ref.3, bf16[16,4096]{1,0:T(8,128)(2,1)} %reshape.29.pool_ref), custom_call_target="tpu_custom_call" | custom-call | tf_op jit(solution)/shard_map/outgoing_rows/pallas_call | solution.py:249
  4.6 23.0 %all_to_all.20 = bf16[32,16,512]{2,1,0:T(8,128)(2,1)} all-to-all(bf16[32,16,512]{2,1,0:T(8,128)(2,1)} %get-tuple-element.17), channel_id=1, replica_groups=mesh['dp'=16,'tensor'=2] {'dp','tensor'}, dimensions={0} | all-to-all | bytes 1048576 | tf_op jit(solution)/shard_map/all_to_all | solution.py:261
  27.7 2.8 %all-to-all-start = ((bf16[32,16,512]{2,1,0:T(8,128)(2,1)}), bf16[32,16,512]{2,1,0:T(8,128)(2,1)S(1)}, u32[]{:S(2)}, u32[]{:S(2)}) async-start(bf16[32,16,512]{2,1,0:T(8,128)(2,1)} %get-tuple-element.16), calls=%async_computation | async-start | bytes 1048576 | tf_op jit(solution)/shard_map/all_to_all | solution.py:261
  30.5 2.6 %reshape.31.refs_4_.refs_5_ = bf16[2,256,1024]{2,1,0:T(8,128)(2,1)} reshape(bf16[2,256,2,512]{3,2,1,0:T(2,128)(2,1)} %param.8) | data formatting | bytes 2097152 | tf_op jit(solution)/shard_map/reshape | solution.py:265
  33.0 13.5 %attention_grads.2 = (bf16[2,256,4096]{2,1,0:T(8,128)(2,1)}, bf16[2,256,4096]{2,1,0:T(8,128)(2,1)}, bf16[2,256,512]{2,1,0:T(8,128)(2,1)}, bf16[2,256,512]{2,1,0:T(8,128)(2,1)}, bf16[512,512]{1,0:T(8,128)(2,1)}) custom-call(s32[2]{0:T(128)} %refs_0_.3, bf16[2,256,4096]{2,1,0:T(8,128)(2,1)} %refs_1_.3, bf16[2,256,4096]{2,1,0:T(8,128)(2,1)} %refs_2_.3, ...), custom_call_target="tpu_custom_call" | custom-call | flops 9663676416 | bytes 8388608 | tf_op jit(solution)/shard_map/attention_grads/pallas_call | solution.py:151
  46.5 0.0 all-to-all-done
  46.6 0.0 copy-start.1
  46.6 0.8 copy-done.1
  47.4 13.7 %attention_grads.3 = (bf16[2,256,4096]{2,1,0:T(8,128)(2,1)}, bf16[2,256,4096]{2,1,0:T(8,128)(2,1)}, bf16[2,256,512]{2,1,0:T(8,128)(2,1)}, bf16[2,256,512]{2,1,0:T(8,128)(2,1)}, bf16[512,512]{1,0:T(8,128)(2,1)}) custom-call(s32[2]{0:T(128)} %refs_0_.3, ...), custom_call_target="tpu_custom_call", output_to_operand_aliasing={{0}: (6, {}), {1}: (7, {}), {2}: (8, {}), {3}: (9, {})} | custom-call | flops 9663676416 | bytes 8388608 | tf_op jit(solution)/shard_map/attention_grads/pallas_call | solution.py:151
  61.1 39.4 %all_to_all.21.refs_1_ = bf16[32,16,512]{2,1,0:T(8,128)(2,1)} all-to-all(bf16[32,16,512]{2,1,0:T(8,128)(2,1)} %bitcast.8), channel_id=1, replica_groups=mesh['dp'=16,'tensor'=2] {'dp','tensor'}, dimensions={0} | all-to-all | bytes 1048576 | tf_op jit(solution)/shard_map/all_to_all | solution.py:274
  100.5 2.8 %all-to-all-start.2 = ((bf16[32,16,512]{2,1,0:T(8,128)(2,1)}), bf16[32,16,512]{2,1,0:T(8,128)(2,1)S(1)}, u32[]{:S(2)}, u32[]{:S(2)}) async-start(bf16[32,16,512]{2,1,0:T(8,128)(2,1)} %bitcast.4), calls=%async_computation.2 | async-start | bytes 1048576 | tf_op jit(solution)/shard_map/all_to_all | solution.py:274
  103.3 1.3 %pad_maximum_fusion = bf16[2,256,2,512]{3,1,0,2:T(8,128)(2,1)S(1)} fusion(bf16[2,256,1,512]{3,1,0,2:T(8,128)(2,1)} %bitcast.10, bf16[2,256,1,512]{3,1,0,2:T(8,128)(2,1)} %bitcast.9), kind=kLoop, calls=%fused_computation | loop fusion | flops 524288 | bytes 2097152 | tf_op jit(solution)/shard_map/stack | solution.py:277
  104.6 2.0 %copy.15 = bf16[2,256,2,512]{3,2,1,0:T(2,128)(2,1)} copy(bf16[2,256,2,512]{3,1,0,2:T(8,128)(2,1)S(1)} %pad_maximum_fusion) | data formatting | bytes 2097152
  106.7 12.5 %all-to-all-done.2.refs_0_ = bf16[32,16,512]{2,1,0:T(8,128)(2,1)S(1)} async-done(((bf16[32,16,512]{2,1,0:T(8,128)(2,1)}), bf16[32,16,512]{2,1,0:T(8,128)(2,1)S(1)}, u32[]{:S(2)}, u32[]{:S(2)}) %all-to-all-start.2) | async-done | bytes 524320 | tf_op jit(solution)/shard_map/all_to_all | solution.py:274
  119.1 0.0 copy-start
  119.1 0.8 copy-done
  119.9 2.0 %prefix_totals.1 = bf16[16,4096]{1,0:T(8,128)(2,1)} custom-call(s32[2,8]{1,0:T(2,128)} %member_ref.3, s32[2]{0:T(128)} %slot_ref.3, bf16[32,16,512]{2,1,0:T(8,128)(2,1)} %copy-done, bf16[32,16,512]{2,1,0:T(8,128)(2,1)} %all_to_all.21.refs_1_), custom_call_target="tpu_custom_call" | custom-call | tf_op jit(solution)/shard_map/prefix_totals/pallas_call | solution.py:279
  122.0 1.6 %reshape.35 = bf16[16,2,2,1024]{3,2,1,0:T(2,128)(2,1)} reshape(bf16[16,4096]{1,0:T(8,128)(2,1)} %prefix_totals.1) | data formatting | bytes 262144 | tf_op jit(solution)/shard_map/reshape | solution.py:287
Async XLA Ops:
  27.7 18.9 %all-to-all-start = ((bf16[32,16,512]{2,1,0:T(8,128)(2,1)}), bf16[32,16,512]{2,1,0:T(8,128)(2,1)S(1)}, u32[]{:S(2)}, u32[]{:S(2)}) async-start(bf16[32,16,512]{2,1,0:T(8,128)(2,1)} %get-tuple-element.16), calls=%async_computation | async-start | bytes 1048576 | tf_op jit(solution)/shard_map/all_to_all | solution.py:261
  46.6 0.8 copy-start.1
  100.5 18.6 %all-to-all-start.2 = ((bf16[32,16,512]{2,1,0:T(8,128)(2,1)}), bf16[32,16,512]{2,1,0:T(8,128)(2,1)S(1)}, u32[]{:S(2)}, u32[]{:S(2)}) async-start(bf16[32,16,512]{2,1,0:T(8,128)(2,1)} %bitcast.4), calls=%async_computation.2 | async-start | bytes 1048576 | tf_op jit(solution)/shard_map/all_to_all | solution.py:274
  119.1 0.8 copy-start

commit v3 on v2

--- a/solution.py
+++ b/solution.py
@@ -89,11 +89,16 @@
         for j, s in enumerate(c["columns"]):
             dquery_ref[0, c["rows"], s] = result[j * tile_rows : (j + 1) * tile_rows]
 
-    def dkey_dvalue(c):
-        dkeys[:, : c["count"]] += dot(c["query"], c["dscore"], TN)
-        dvalues[:, : c["count"]] += dot(c["grad"], c["exps"], TN)
-
-    stages = (score, softmax, attend, dscore, dquery, dkey_dvalue)
+    def dkey_dvalue(chains):
+        count = chains[0]["count"]
+        query, dscores, grad, exps = (
+            jnp.concatenate([c.pop(name) for c in chains], 0)
+            for name in ("query", "dscore", "grad", "exps")
+        )
+        dkeys[:, :count] += dot(query, dscores, TN)
+        dvalues[:, :count] += dot(grad, exps, TN)
+
+    stages = (score, softmax, attend, dscore, dquery)
 
     def work(tiles):
         chains = [
@@ -110,6 +115,8 @@
             for i, chain in enumerate(chains):
                 if 0 <= step - i < len(stages):
                     stages[step - i](chain)
+        for t in tiles:
+            dkey_dvalue([c for c in chains if c["first_row"] == t])
 
     starts = list(range(0, row_count, tile_rows))
     for k in range(len(starts)):
@@ -180,53 +187,68 @@
     )(resp_len, queries, grad_out, prefix, own_kv, own_kv, *held)
 
 
-def outgoing_kernel(shape, chunks, member_ref, slot_ref, pool_ref, *out_refs):
-    tensor_count, kv_local = shape
+def outgoing_kernel(tensor_count, kv_local, base, member_ref, slot_ref, pool_ref, out_ref, flat):
     prompts, members = member_ref.shape
-    kv_width = kv_local * HEAD
-    half = tensor_count * kv_width
+    heads = out_ref.shape[2] // (2 * HEAD)
+    half = tensor_count * kv_local * HEAD
+    for slot in range(pool_ref.shape[1]):
+        for part in range(2):
+            flat[:, (2 * slot + part) * half : (2 * slot + part + 1) * half] = pool_ref[
+                :, slot, part, :
+            ]
 
     def one(i, carry):
         prompt = i // members
         owner = member_ref[prompt, i % members]
-        start = pl.multiple_of(slot_ref[prompt] * 2 * half, HEAD)
+        start = slot_ref[prompt] * 2 * half
         for t in range(tensor_count):
-            for (base, heads), out_ref in zip(chunks, out_refs):
-                for h in range(heads):
-                    for part in range(2):
-                        source = part * half + t * kv_width + (base + h) * HEAD
-                        out_ref[owner * tensor_count + t, :, pl.ds((2 * h + part) * HEAD, HEAD)] = (
-                            pool_ref[:, pl.ds(pl.multiple_of(start + source, HEAD), HEAD)]
-                        )
+            for h in range(heads):
+                for part in range(2):
+                    source = start + part * half + (t * kv_local + base + h) * HEAD
+                    out_ref[owner * tensor_count + t, :, pl.ds((2 * h + part) * HEAD, HEAD)] = flat[
+                        :, pl.ds(pl.multiple_of(source, HEAD), HEAD)
+                    ]
         return carry
 
     lax.fori_loop(0, prompts * members, one, 0)
 
 
-def total_kernel(shape, chunks, member_ref, slot_ref, *refs):
-    tensor_count, kv_local = shape
-    in_refs, out_ref = refs[:-1], refs[-1]
+def total_kernel(tensor_count, kv_local, base, member_ref, slot_ref, in_ref, *refs):
     prompts, members = member_ref.shape
-    kv_width = kv_local * HEAD
-    half = tensor_count * kv_width
+    heads = in_ref.shape[2] // (2 * HEAD)
+    half = tensor_count * kv_local * HEAD
+    flat = refs[-1]
+    if len(refs) == 3:
+        flat[...] = refs[0][...]
 
     def one(prompt, carry):
-        start = pl.multiple_of(slot_ref[prompt] * 2 * half, HEAD)
-        for (base, heads), in_ref in zip(chunks, in_refs):
-            for t in range(tensor_count):
-                total = in_ref[member_ref[prompt, 0] * tensor_count + t].astype(F32)
-                for m in range(1, members):
-                    total += in_ref[member_ref[prompt, m] * tensor_count + t].astype(F32)
-                total = total.astype(BF16)
-                for h in range(heads):
-                    for part in range(2):
-                        target = part * half + t * kv_width + (base + h) * HEAD
-                        out_ref[:, pl.ds(pl.multiple_of(start + target, HEAD), HEAD)] = total[
-                            :, (2 * h + part) * HEAD : (2 * h + part + 1) * HEAD
-                        ]
+        start = slot_ref[prompt] * 2 * half
+        for t in range(tensor_count):
+            total = in_ref[member_ref[prompt, 0] * tensor_count + t].astype(F32)
+            for m in range(1, members):
+                total += in_ref[member_ref[prompt, m] * tensor_count + t].astype(F32)
+            total = total.astype(BF16)
+            for h in range(heads):
+                for part in range(2):
+                    target = start + part * half + (t * kv_local + base + h) * HEAD
+                    flat[:, pl.ds(pl.multiple_of(target, HEAD), HEAD)] = total[
+                        :, (2 * h + part) * HEAD : (2 * h + part + 1) * HEAD
+                    ]
         return carry
 
     lax.fori_loop(0, prompts, one, 0)
+    if len(refs) > 1:
+        out_ref = refs[-2]
+        for slot in range(out_ref.shape[1]):
+            for part in range(2):
+                out_ref[:, slot, part, :] = flat[
+                    :, (2 * slot + part) * half : (2 * slot + part + 1) * half
+                ]
+
+
+def exchange(block, after):
+    block, *after = lax.optimization_barrier((block, *after))
+    return lax.all_to_all(block, EVERYONE, split_axis=0, concat_axis=0, tiled=True), after
 
 
 SMEM = pl.BlockSpec(memory_space=pltpu.SMEM)
@@ -245,46 +267,57 @@
     first = (kv_local + 1) // 2
     chunks = [(0, first)] + ([(first, kv_local - first)] if first < kv_local else [])
     params = pltpu.CompilerParams(vmem_limit_bytes=VMEM_LIMIT)
-
-    outgoing = pl.pallas_call(
-        functools.partial(outgoing_kernel, shape, chunks),
-        in_specs=[SMEM, SMEM, VMEM],
-        out_specs=[VMEM] * len(chunks),
-        out_shape=[
-            jax.ShapeDtypeStruct((devices, slice_rows, 2 * HEAD * heads), BF16)
-            for _, heads in chunks
-        ],
-        compiler_params=params,
-        name="outgoing_rows",
-    )(member_list, prompt_slot, prefix_pool.reshape(slice_rows, -1))
-    prefixes = [
-        lax.all_to_all(block, EVERYONE, split_axis=0, concat_axis=0, tiled=True)
-        for block in outgoing
-    ]
+    pool_width = prefix_pool.size // slice_rows
+
+    def outgoing(base, heads, pool):
+        return pl.pallas_call(
+            functools.partial(outgoing_kernel, *shape, base),
+            in_specs=[SMEM, SMEM, VMEM],
+            out_specs=VMEM,
+            out_shape=jax.ShapeDtypeStruct((devices, slice_rows, 2 * HEAD * heads), BF16),
+            scratch_shapes=[pltpu.VMEM((slice_rows, pool_width), BF16)],
+            compiler_params=params,
+            name="outgoing_rows",
+        )(member_list, prompt_slot, pool)
+
+    def totals(base, block, flat, last):
+        held = [] if flat is None else [flat]
+        flat_shape = jax.ShapeDtypeStruct((slice_rows, pool_width), BF16)
+        return pl.pallas_call(
+            functools.partial(total_kernel, *shape, base),
+            in_specs=[SMEM, SMEM, VMEM] + [VMEM] * len(held),
+            out_specs=VMEM,
+            out_shape=jax.ShapeDtypeStruct(prefix_pool.shape, BF16) if last else flat_shape,
+            scratch_shapes=[pltpu.VMEM(flat_shape.shape, BF16)] if last else [],
+            compiler_params=params,
+            name="prefix_totals",
+        )(member_list, prompt_slot, block, *held)
 
     own_kv = resp_kv.reshape(responses, rows, 2 * kv_width)
-    held, arrived = [], []
-    for (base, heads), prefix in zip(chunks, prefixes):
+    prefix, _ = exchange(outgoing(*chunks[0], prefix_pool), ())
+    held, flat, arrived = [], None, None
+    for k, (base, heads) in enumerate(chunks):
+        last = k + 1 == len(chunks)
+        if not last:
+            ahead = outgoing(*chunks[k + 1], prefix_pool)
+            coming, (prefix, own_kv) = exchange(ahead, (prefix, own_kv))
         prefix = prefix.reshape(devices * slice_rows, 2 * HEAD * heads)
         *held, far_grad = attention_grads(
             queries, grad_out, own_kv, prefix, resp_len, base, held
         )
         far_grad = far_grad.reshape(devices, slice_rows, 2 * HEAD * heads)
-        arrived.append(
-            lax.all_to_all(far_grad, EVERYONE, split_axis=0, concat_axis=0, tiled=True)
-        )
+        if arrived is None:
+            arrived, _ = exchange(far_grad, ())
+        else:
+            following, (arrived,) = exchange(far_grad, (arrived,))
+            flat = totals(chunks[k - 1][0], arrived, flat, False)
+            arrived = following
+        if not last:
+            prefix = coming
     attention, grad_queries, own_dkey, own_dvalue = held
     grad_resp_kv = jnp.stack([own_dkey, own_dvalue], axis=2)
-
-    grad_prefix = pl.pallas_call(
-        functools.partial(total_kernel, shape, chunks),
-        in_specs=[SMEM, SMEM] + [VMEM] * len(chunks),
-        out_specs=VMEM,
-        out_shape=jax.ShapeDtypeStruct((slice_rows, prefix_pool.size // slice_rows), BF16),
-        compiler_params=params,
-        name="prefix_totals",
-    )(member_list, prompt_slot, *arrived)
-    return attention, grad_queries, grad_resp_kv, grad_prefix.reshape(prefix_pool.shape)
+    grad_prefix = totals(chunks[-1][0], arrived, flat, True)
+    return attention, grad_queries, grad_resp_kv, grad_prefix
 
 
 def solution(mesh):

time: 124 us -> 104 us (0.84)
  blocking collectives: 62.5 us -> 0 us
  starting transfers between devices: 5.61 us -> 34.3 us
  waiting for transfers between devices: 12.5 us -> 26.2 us
  local copies, waits for them, and re-layouts: 9.5 us -> 5.42 us
  Pallas kernels: 31.6 us -> 35.3 us
    all_to_all x2 -> x0, blocking collectives: 62.5 us -> none  [the longest x1 39.4 us: on_device(): lax.all_to_all(far_grad, EVERYONE, split_axis=0, concat_axis=0, tiled=True)]
    all_to_all x2 -> x4, starting transfers between devices: 5.61 us -> 34.3 us  [exchange(): lax.all_to_all(block, EVERYONE, split_axis=0, concat_axis=0, tiled=True)]
    all_to_all x2 -> x4, waiting for transfers between devices: 12.5 us -> 26.2 us  [exchange(): lax.all_to_all(block, EVERYONE, split_axis=0, concat_axis=0, tiled=True)]
    pallas_call x2 -> x4, Pallas kernels: 4.39 us -> 8.37 us  [the longest x2 4.72 us: outgoing(): pl.pallas_call(functools.partial(outgoing_kernel, *shape, base), in_specs...]
    reshape x2 -> x0, local copies, waits for them, and re-layouts: 3.27 us -> none  [the longest x1 1.64 us: on_device(): grad_prefix.reshape(prefix_pool.shape)]
    unnamed x5 -> x9, local copies, waits for them, and re-layouts: 3.66 us -> 2.86 us
  transfers between devices with their start and end apart: 2 -> 4, of which waited for: 1 -> 4; matrix products, arithmetic and copies ran while one was open for 5% -> 6% of each run, Pallas kernels for 11% -> 30%
where the time goes in v3:
time: 104 us; the launch traced here: 103 us
  Pallas kernels  35.3 us (34%)
  starting transfers between devices  34.3 us (33%)
  waiting for transfers between devices  26.2 us (25%)
  local copies, waits for them, and re-layouts  5.42 us (5%)
  other arithmetic  1.3 us (1%)
    all_to_all x4, starting transfers between devices, exchange(): lax.all_to_all(block, EVERYONE, split_axis=0, concat_axis=0, tiled=True)  34.3 us
    pallas_call x2, Pallas kernels, attention_grads(): pl.pallas_call(functools.partial(attention_kernel, tile_rows, head_block,...  26.9 us
    all_to_all x4, waiting for transfers between devices, exchange(): lax.all_to_all(block, EVERYONE, split_axis=0, concat_axis=0, tiled=True)  26.2 us
    pallas_call x2, Pallas kernels, outgoing(): pl.pallas_call(functools.partial(outgoing_kernel, *shape, base), in_specs...  4.72 us
    pallas_call x2, Pallas kernels, totals(): pl.pallas_call(functools.partial(total_kernel, *shape, base), in_specs=[S...  3.65 us
    unnamed x9, local copies, waits for them, and re-layouts  2.86 us
    reshape x1, local copies, waits for them, and re-layouts, on_device(): own_kv = resp_kv.reshape(responses, rows, 2 * kv_width)  2.57 us
  transfers between devices with their start and end apart: 4, of which 4 were waited for; matrix products, arithmetic and copies ran while one was open for 6% of the time, Pallas kernels for 30%

profile of v3, /device:TPU:1, one launch (start us, length us, event | category | flops | bytes accessed | tf_op | source)
XLA Modules:
  0.0 103.3 jit_solution(18408248010260403784)
XLA Ops:
  0.6 2.4 %outgoing_rows.3 = bf16[32,16,512]{2,1,0:T(8,128)(2,1)} custom-call(s32[2,8]{1,0:T(2,128)} %member_ref.7, s32[2]{0:T(128)} %slot_ref.7, bf16[16,2,2,1024]{3,2,1,0:T(2,128)(2,1)} %pool_ref.3), custom_call_target="tpu_custom_call" | custom-call | tf_op jit(solution)/shard_map/outgoing_rows/pallas_call | solution.py:273
  3.0 7.1 %all-to-all-start = ((bf16[32,16,512]{2,1,0:T(8,128)(2,1)}), bf16[32,16,512]{2,1,0:T(8,128)(2,1)S(1)}, u32[]{:S(2)}, u32[]{:S(2)}) async-start(bf16[32,16,512]{2,1,0:T(8,128)(2,1)} %outgoing_rows.3), calls=%async_computation | async-start | bytes 1048576 | tf_op jit(solution)/shard_map/all_to_all | solution.py:251
  10.1 2.4 %outgoing_rows.2 = bf16[32,16,512]{2,1,0:T(8,128)(2,1)} custom-call(s32[2,8]{1,0:T(2,128)} %member_ref.7, s32[2]{0:T(128)} %slot_ref.7, bf16[16,2,2,1024]{3,2,1,0:T(2,128)(2,1)} %pool_ref.3), custom_call_target="tpu_custom_call" | custom-call | tf_op jit(solution)/shard_map/outgoing_rows/pallas_call | solution.py:273
  12.5 2.6 %reshape.23.refs_4_.refs_5_ = bf16[2,256,1024]{2,1,0:T(8,128)(2,1)} reshape(bf16[2,256,2,512]{3,2,1,0:T(2,128)(2,1)} %param.8) | data formatting | bytes 2097152 | tf_op jit(solution)/shard_map/reshape | solution.py:296
  15.0 10.9 %all-to-all-done = bf16[32,16,512]{2,1,0:T(8,128)(2,1)S(1)} async-done(((bf16[32,16,512]{2,1,0:T(8,128)(2,1)}), bf16[32,16,512]{2,1,0:T(8,128)(2,1)S(1)}, u32[]{:S(2)}, u32[]{:S(2)}) %all-to-all-start) | async-done | bytes 524320 | tf_op jit(solution)/shard_map/all_to_all | solution.py:251
  25.9 0.0 copy-start.3
  25.9 2.8 %all-to-all-start.1 = ((bf16[32,16,512]{2,1,0:T(8,128)(2,1)}), bf16[32,16,512]{2,1,0:T(8,128)(2,1)S(1)}, u32[]{:S(2)}, u32[]{:S(2)}) async-start(bf16[32,16,512]{2,1,0:T(8,128)(2,1)} %outgoing_rows.2), calls=%async_computation.1 | async-start | bytes 1048576 | tf_op jit(solution)/shard_map/all_to_all | solution.py:251
  28.7 0.0 copy-done.3
  28.7 13.5 %attention_grads.2 = (bf16[2,256,4096]{2,1,0:T(8,128)(2,1)}, bf16[2,256,4096]{2,1,0:T(8,128)(2,1)}, bf16[2,256,512]{2,1,0:T(8,128)(2,1)}, bf16[2,256,512]{2,1,0:T(8,128)(2,1)}, bf16[512,512]{1,0:T(8,128)(2,1)}) custom-call(s32[2]{0:T(128)} %refs_0_.3, bf16[2,256,4096]{2,1,0:T(8,128)(2,1)} %refs_1_.3, bf16[2,256,4096]{2,1,0:T(8,128)(2,1)} %refs_2_.3, ...), custom_call_target="tpu_custom_call" | custom-call | flops 9663676416 | bytes 8388608 | tf_op jit(solution)/shard_map/attention_grads/pallas_call | solution.py:158
  42.2 2.3 %all-to-all-done.1 = bf16[32,16,512]{2,1,0:T(8,128)(2,1)S(1)} async-done(((bf16[32,16,512]{2,1,0:T(8,128)(2,1)}), bf16[32,16,512]{2,1,0:T(8,128)(2,1)S(1)}, u32[]{:S(2)}, u32[]{:S(2)}) %all-to-all-start.1) | async-done | bytes 524320 | tf_op jit(solution)/shard_map/all_to_all | solution.py:251
  44.5 0.0 copy-start.2
  44.5 12.2 %all-to-all-start.2 = ((bf16[32,16,512]{2,1,0:T(8,128)(2,1)}), bf16[32,16,512]{2,1,0:T(8,128)(2,1)S(1)}, u32[]{:S(2)}, u32[]{:S(2)}) async-start(bf16[32,16,512]{2,1,0:T(8,128)(2,1)} %bitcast.8), calls=%async_computation.2 | async-start | bytes 1048576 | tf_op jit(solution)/shard_map/all_to_all | solution.py:251
  56.7 0.0 copy-done.2
  56.8 13.5 %attention_grads.3 = (bf16[2,256,4096]{2,1,0:T(8,128)(2,1)}, bf16[2,256,4096]{2,1,0:T(8,128)(2,1)}, bf16[2,256,512]{2,1,0:T(8,128)(2,1)}, bf16[2,256,512]{2,1,0:T(8,128)(2,1)}, bf16[512,512]{1,0:T(8,128)(2,1)}) custom-call(s32[2]{0:T(128)} %refs_0_.3, ...), custom_call_target="tpu_custom_call", output_to_operand_aliasing={{0}: (6, {}), {1}: (7, {}), {2}: (8, {}), {3}: (9, {})} | custom-call | flops 9663676416 | bytes 8388608 | tf_op jit(solution)/shard_map/attention_grads/pallas_call | solution.py:158
  70.2 2.3 %all-to-all-done.2.in_ref = bf16[32,16,512]{2,1,0:T(8,128)(2,1)S(1)} async-done(((bf16[32,16,512]{2,1,0:T(8,128)(2,1)}), bf16[32,16,512]{2,1,0:T(8,128)(2,1)S(1)}, u32[]{:S(2)}, u32[]{:S(2)}) %all-to-all-start.2) | async-done | bytes 524320 | tf_op jit(solution)/shard_map/all_to_all | solution.py:251
  72.6 0.0 copy-start
  72.6 12.2 %all-to-all-start.3 = ((bf16[32,16,512]{2,1,0:T(8,128)(2,1)}), bf16[32,16,512]{2,1,0:T(8,128)(2,1)S(1)}, u32[]{:S(2)}, u32[]{:S(2)}) async-start(bf16[32,16,512]{2,1,0:T(8,128)(2,1)} %bitcast.7), calls=%async_computation.3 | async-start | bytes 1048576 | tf_op jit(solution)/shard_map/all_to_all | solution.py:251
  84.8 0.0 copy-done
  84.8 1.8 %prefix_totals.2.refs_0_ = bf16[16,4096]{1,0:T(8,128)(2,1)} custom-call(s32[2,8]{1,0:T(2,128)} %member_ref.7, s32[2]{0:T(128)} %slot_ref.7, bf16[32,16,512]{2,1,0:T(8,128)(2,1)} %copy-done), custom_call_target="tpu_custom_call" | custom-call | tf_op jit(solution)/shard_map/prefix_totals/pallas_call | solution.py:286
  86.6 1.3 %pad_maximum_fusion = bf16[2,256,2,512]{3,1,0,2:T(8,128)(2,1)S(1)} fusion(bf16[2,256,1,512]{3,1,0,2:T(8,128)(2,1)} %bitcast.11, bf16[2,256,1,512]{3,1,0,2:T(8,128)(2,1)} %bitcast.10), kind=kLoop, calls=%fused_computation | loop fusion | flops 524288 | bytes 2097152 | tf_op jit(solution)/shard_map/stack | solution.py:318
  87.9 2.0 %copy.15 = bf16[2,256,2,512]{3,2,1,0:T(2,128)(2,1)} copy(bf16[2,256,2,512]{3,1,0,2:T(8,128)(2,1)S(1)} %pad_maximum_fusion) | data formatting | bytes 2097152
  89.9 10.7 %all-to-all-done.3.in_ref = bf16[32,16,512]{2,1,0:T(8,128)(2,1)S(1)} async-done(((bf16[32,16,512]{2,1,0:T(8,128)(2,1)}), bf16[32,16,512]{2,1,0:T(8,128)(2,1)S(1)}, u32[]{:S(2)}, u32[]{:S(2)}) %all-to-all-start.3) | async-done | bytes 524320 | tf_op jit(solution)/shard_map/all_to_all | solution.py:251
  100.6 0.0 copy-start.1
  100.6 0.8 copy-done.1
  101.4 1.9 %prefix_totals.3 = bf16[16,2,2,1024]{3,2,1,0:T(2,128)(2,1)} custom-call(s32[2,8]{1,0:T(2,128)} %member_ref.7, s32[2]{0:T(128)} %slot_ref.7, bf16[32,16,512]{2,1,0:T(8,128)(2,1)} %copy-done.1, bf16[16,4096]{1,0:T(8,128)(2,1)} %prefix_totals.2.refs_0_), custom_call_target="tpu_custom_call" | custom-call | tf_op jit(solution)/shard_map/prefix_totals/pallas_call | solution.py:286
Async XLA Ops:
  3.0 22.9 %all-to-all-start = ((bf16[32,16,512]{2,1,0:T(8,128)(2,1)}), bf16[32,16,512]{2,1,0:T(8,128)(2,1)S(1)}, u32[]{:S(2)}, u32[]{:S(2)}) async-start(bf16[32,16,512]{2,1,0:T(8,128)(2,1)} %outgoing_rows.3), calls=%async_computation | async-start | bytes 1048576 | tf_op jit(solution)/shard_map/all_to_all | solution.py:251
  25.9 2.8 %copy-start.3 = (bf16[32,16,512]{2,1,0:T(8,128)(2,1)}, bf16[32,16,512]{2,1,0:T(8,128)(2,1)S(1)}, u32[]{:S(2)}) copy-start(bf16[32,16,512]{2,1,0:T(8,128)(2,1)S(1)} %all-to-all-done) | copy-start | bytes 1572868
  25.9 18.6 %all-to-all-start.1 = ((bf16[32,16,512]{2,1,0:T(8,128)(2,1)}), bf16[32,16,512]{2,1,0:T(8,128)(2,1)S(1)}, u32[]{:S(2)}, u32[]{:S(2)}) async-start(bf16[32,16,512]{2,1,0:T(8,128)(2,1)} %outgoing_rows.2), calls=%async_computation.1 | async-start | bytes 1048576 | tf_op jit(solution)/shard_map/all_to_all | solution.py:251
  44.5 12.2 %copy-start.2 = (bf16[32,16,512]{2,1,0:T(8,128)(2,1)}, bf16[32,16,512]{2,1,0:T(8,128)(2,1)S(1)}, u32[]{:S(2)}) copy-start(bf16[32,16,512]{2,1,0:T(8,128)(2,1)S(1)} %all-to-all-done.1) | copy-start | bytes 1572868
  44.5 28.0 %all-to-all-start.2 = ((bf16[32,16,512]{2,1,0:T(8,128)(2,1)}), bf16[32,16,512]{2,1,0:T(8,128)(2,1)S(1)}, u32[]{:S(2)}, u32[]{:S(2)}) async-start(bf16[32,16,512]{2,1,0:T(8,128)(2,1)} %bitcast.8), calls=%async_computation.2 | async-start | bytes 1048576 | tf_op jit(solution)/shard_map/all_to_all | solution.py:251
  72.6 12.2 %copy-start = (bf16[32,16,512]{2,1,0:T(8,128)(2,1)}, bf16[32,16,512]{2,1,0:T(8,128)(2,1)S(1)}, u32[]{:S(2)}) copy-start(bf16[32,16,512]{2,1,0:T(8,128)(2,1)S(1)} %all-to-all-done.2.in_ref) | copy-start | bytes 1572868
  72.6 28.0 %all-to-all-start.3 = ((bf16[32,16,512]{2,1,0:T(8,128)(2,1)}), bf16[32,16,512]{2,1,0:T(8,128)(2,1)S(1)}, u32[]{:S(2)}, u32[]{:S(2)}) async-start(bf16[32,16,512]{2,1,0:T(8,128)(2,1)} %bitcast.7), calls=%async_computation.3 | async-start | bytes 1048576 | tf_op jit(solution)/shard_map/all_to_all | solution.py:251
  100.6 0.8 copy-start.1

commit v4 on v3

v4 whole, which is shorter than its diff:
```python
import functools
import math

import jax
import jax.numpy as jnp
from jax import lax
from jax.experimental import pallas as pl
from jax.experimental.pallas import tpu as pltpu
from jax.sharding import PartitionSpec as P

HEAD = 128
F32 = jnp.float32
BF16 = jnp.bfloat16
SCALE = HEAD ** (-0.5)
LOG2_SCALE = SCALE * math.log2(math.e)
NT = ((1,), (1,))
NN = ((1,), (0,))
TN = ((0,), (0,))
EVERYONE = ("dp", "tensor")
VMEM_LIMIT = 56 << 20


def dot(a, b, dims):
    return lax.dot_general(a, b, (dims, ((), ())), preferred_element_type=F32)


def attention_kernel(tile_rows, head_block, group, *refs):
    len_ref, query_ref, grad_ref, far_ref, own_key_ref, own_value_ref = refs[:6]
    out_ref, dquery_ref, own_dkey_ref, own_dvalue_ref, far_grad_ref = refs[-9:-4]
    keys, values, dkeys, dvalues = refs[-4:]
    responses, row_count = query_ref.shape[:2]
    prompt_rows = far_ref.shape[0]
    tall = head_block * tile_rows

    def hold(r, rows, key, value):
        keys[r, rows, :HEAD] = key
        keys[r, rows, HEAD:] = key
        values[r, rows, :] = value

    for r in range(responses):
        hold(r, pl.ds(0, prompt_rows), far_ref[:, :HEAD], far_ref[:, HEAD:])
        hold(r, pl.ds(prompt_rows, row_count), own_key_ref[r], own_value_ref[r])

    def score(c):
        r = c["response"]
        c["query"] = jnp.concatenate([query_ref[r, c["rows"], s] for s in c["columns"]], 0)
        scaled = c["query"].astype(F32) * LOG2_SCALE
        high = scaled.astype(BF16)
        low = (scaled - high.astype(F32)).astype(BF16)
        c["score"] = dot(jnp.concatenate([high, low], 1), keys[r, : c["count"]], NT)

    def softmax(c):
        scores, count = c.pop("score"), c["count"]
        row = lax.broadcasted_iota(jnp.int32, (tall, tile_rows), 0) % tile_rows
        column = lax.broadcasted_iota(jnp.int32, (tall, tile_rows), 1)
        corner = jnp.where(column <= row, scores[:, count - tile_rows :], -jnp.inf)
        scores = jnp.concatenate([scores[:, : count - tile_rows], corner], 1)
        exps = jnp.exp2(scores - jnp.max(scores, 1, keepdims=True))
        c["exps"] = exps.astype(BF16)
        place = lax.broadcasted_iota(jnp.int32, (tall, 1), 0) % tile_rows + c["first_row"]
        c["inverse"] = jnp.where(
            place < len_ref[c["response"]], 1.0 / jnp.sum(exps, 1, keepdims=True), 0.0
        )

    def attend(c):
        r = c["response"]
        inverse, value = c.pop("inverse"), values[r, : c["count"]]
        out = (dot(c["exps"], value, NN) * inverse).astype(BF16)
        grad = jnp.concatenate([grad_ref[r, c["rows"], s] for s in c["columns"]], 0)
        c["grad"] = grad = (grad.astype(F32) * inverse).astype(BF16)
        c["delta"] = jnp.sum(grad.astype(F32) * out.astype(F32), 1, keepdims=True)
        for j, s in enumerate(c["columns"]):
            out_ref[r, c["rows"], s] = out[j * tile_rows : (j + 1) * tile_rows]
        c["dprobs"] = dot(grad, value, NT)

    def dscore(c):
        c["dscore"] = c["exps"] * (c.pop("dprobs") - c.pop("delta")).astype(BF16)

    def dquery(c):
        r = c["response"]
        result = (dot(c["dscore"], keys[r, : c["count"], :HEAD], NN) * SCALE).astype(BF16)
        for j, s in enumerate(c["columns"]):
            dquery_ref[r, c["rows"], s] = result[j * tile_rows : (j + 1) * tile_rows]

    def dkey_dvalue(chains, opening):
        r, count = chains[0]["response"], chains[0]["count"]
        query, dscores, grad, exps = (
            jnp.concatenate([c.pop(name) for c in chains], 0)
            for name in ("query", "dscore", "grad", "exps")
        )
        for ref, block in ((dkeys, dot(query, dscores, TN)), (dvalues, dot(grad, exps, TN))):
            if not opening:
                ref[r, :, :count] += block
                continue
            ref[r, :, :count] = block
            if count < ref.shape[2]:
                ref[r, :, count:] = jnp.zeros((HEAD, ref.shape[2] - count), F32)

    stages = (score, softmax, attend, dscore, dquery)
    blocks = group // head_block

    def work(which, tiles):
        chains = [
            {
                "response": r,
                "columns": [
                    pl.ds((h * head_block + j) * HEAD, HEAD) for j in range(head_block)
                ],
                "rows": pl.ds(t, tile_rows),
                "first_row": t,
                "count": prompt_rows + t + tile_rows,
            }
            for r in which
            for t in reversed(tiles)
            for h in range(blocks)
        ]
        for step in range(len(stages) + len(chains) - 1):
            for i, chain in enumerate(chains):
                if 0 <= step - i < len(stages):
                    stages[step - i](chain)
            ended = step - len(stages) + 2
            if ended > 0 and ended % blocks == 0:
                whole_tile = chains[ended - blocks : ended]
                dkey_dvalue(whole_tile, whole_tile[0]["first_row"] == tiles[-1])

    starts = list(range(0, row_count, tile_rows))
    shortest = len_ref[0]
    for r in range(1, responses):
        shortest = jnp.minimum(shortest, len_ref[r])

    @pl.when(shortest > starts[-1])
    def _():
        work(range(responses), starts)

    @pl.when(shortest <= starts[-1])
    def _():
        def one(r, carry):
            live_count = len_ref[r]
            for k in range(len(starts)):
                last = k + 1 == len(starts)
                upper = row_count if last else starts[k + 1]

                @pl.when((live_count > starts[k]) & (last | (live_count <= upper)))
                def _(k=k, last=last, upper=upper):
                    work([r], starts[: k + 1])
                    if not last:
                        blank = jnp.zeros((row_count - upper, group * HEAD), BF16)
                        out_ref[r, upper:, :] = blank
                        dquery_ref[r, upper:, :] = blank

            return carry

        lax.fori_loop(0, responses, one, 0)

    for r in range(responses):
        own_dkey_ref[r] = (dkeys[r, :, prompt_rows:] * SCALE).astype(BF16).T
        own_dvalue_ref[r] = dvalues[r, :, prompt_rows:].astype(BF16).T
    far = pl.ds(0, prompt_rows)
    far_dkey, far_dvalue = dkeys[0, :, far], dvalues[0, :, far]
    for r in range(1, responses):
        far_dkey += dkeys[r, :, far]
        far_dvalue += dvalues[r, :, far]
    far_grad_ref[:, :HEAD] = (far_dkey * SCALE).astype(BF16).T
    far_grad_ref[:, HEAD:] = far_dvalue.astype(BF16).T


def attention_grads(queries, grad_out, own_kv, prefix, resp_len, base, held):
    responses, rows, width = queries.shape
    kv_local = own_kv.shape[2] // (2 * HEAD)
    group = width // HEAD // kv_local
    prompt_rows = prefix.shape[0]
    heads = prefix.shape[1] // (2 * HEAD)
    tile_rows = min(128, rows)
    head_block = math.gcd(group, 4)
    wide = pl.BlockSpec((responses, rows, group * HEAD), lambda a, *_: (0, 0, a + base))
    own_k = pl.BlockSpec((responses, rows, HEAD), lambda a, *_: (0, 0, a + base))
    own_v = pl.BlockSpec((responses, rows, HEAD), lambda a, *_: (0, 0, a + base + kv_local))
    far = pl.BlockSpec((prompt_rows, 2 * HEAD), lambda a, *_: (0, a))
    anywhere = pl.BlockSpec(memory_space=pl.ANY)
    own_shape = jax.ShapeDtypeStruct((responses, rows, kv_local * HEAD), BF16)
    pairs = responses * rows * group * heads * (prompt_rows + rows)
    return pl.pallas_call(
        functools.partial(attention_kernel, tile_rows, head_block, group),
        grid_spec=pltpu.PrefetchScalarGridSpec(
            num_scalar_prefetch=1,
            grid=(heads,),
            in_specs=[wide, wide, far, own_k, own_v] + [anywhere] * len(held),
            out_specs=[wide, wide, own_k, own_k, far],
            scratch_shapes=[
                pltpu.VMEM((responses, prompt_rows + rows, 2 * HEAD), BF16),
                pltpu.VMEM((responses, prompt_rows + rows, HEAD), BF16),
                pltpu.VMEM((responses, HEAD, prompt_rows + rows), F32),
                pltpu.VMEM((responses, HEAD, prompt_rows + rows), F32),
            ],
        ),
        out_shape=[
            jax.ShapeDtypeStruct(queries.shape, BF16),
            jax.ShapeDtypeStruct(queries.shape, BF16),
            own_shape,
            own_shape,
            jax.ShapeDtypeStruct(prefix.shape, BF16),
        ],
        input_output_aliases={6 + i: i for i in range(len(held))},
        compiler_params=pltpu.CompilerParams(vmem_limit_bytes=VMEM_LIMIT),
        cost_estimate=pl.CostEstimate(
            flops=12 * HEAD * pairs,
            transcendentals=pairs,
            bytes_accessed=8 * responses * rows * group * heads * HEAD,
        ),
        name="attention_grads",
    )(resp_len, queries, grad_out, prefix, own_kv, own_kv, *held)


def outgoing_kernel(tensor_count, kv_local, base, member_ref, slot_ref, pool_ref, out_ref, flat):
    prompts, members = member_ref.shape
    heads = out_ref.shape[2] // (2 * HEAD)
    width = 2 * heads * HEAD
    for slot in range(pool_ref.shape[1]):
        for t in range(tensor_count):
            source = (t * kv_local + base) * HEAD
            for h in range(heads):
                for part in range(2):
                    target = (slot * tensor_count + t) * width + (2 * h + part) * HEAD
                    flat[:, target : target + HEAD] = pool_ref[
                        :, slot, part, source + h * HEAD : source + (h + 1) * HEAD
                    ]

    def one(i, carry):
        prompt = i // members
        owner = member_ref[prompt, i % members]
        for t in range(tensor_count):
            start = pl.multiple_of((slot_ref[prompt] * tensor_count + t) * width, HEAD)
            out_ref[owner * tensor_count + t] = flat[:, pl.ds(start, width)]
        return carry

    lax.fori_loop(0, prompts * members, one, 0)


def total_kernel(tensor_count, kv_local, base, member_ref, slot_ref, in_ref, *refs):
    prompts, members = member_ref.shape
    heads = in_ref.shape[2] // (2 * HEAD)
    out_ref = refs[-1]
    if len(refs) > 1:
        out_ref[...] = refs[0][...]

    def one(prompt, carry):
        for t in range(tensor_count):
            total = in_ref[member_ref[prompt, 0] * tensor_count + t].astype(F32)
            for m in range(1, members):
                total += in_ref[member_ref[prompt, m] * tensor_count + t].astype(F32)
            total = total.astype(BF16)
            for h in range(heads):
                for part in range(2):
                    target = (t * kv_local + base + h) * HEAD
                    out_ref[:, slot_ref[prompt], part, target : target + HEAD] = total[
                        :, (2 * h + part) * HEAD : (2 * h + part + 1) * HEAD
                    ]
        return carry

    lax.fori_loop(0, prompts, one, 0)


def exchange(block, after):
    block, *after = lax.optimization_barrier((block, *after))
    return lax.all_to_all(block, EVERYONE, split_axis=0, concat_axis=0, tiled=True), after


SMEM = pl.BlockSpec(memory_space=pltpu.SMEM)
VMEM = pl.BlockSpec(memory_space=pltpu.VMEM)


def on_device(queries, resp_kv, prefix_pool, grad_out, member_list, prompt_slot, resp_len):
    dp_count = lax.axis_size("dp")
    tensor_count = lax.axis_size("tensor")
    devices = dp_count * tensor_count
    responses, rows = queries.shape[:2]
    kv_width = resp_kv.shape[3]
    kv_local = kv_width // HEAD
    slice_rows, slot_count = prefix_pool.shape[:2]
    shape = (tensor_count, kv_local)
    first = (kv_local + 1) // 2
    chunks = [(0, first)] + ([(first, kv_local - first)] if first < kv_local else [])
    params = pltpu.CompilerParams(vmem_limit_bytes=VMEM_LIMIT)

    def outgoing(base, heads, pool):
        width = slot_count * tensor_count * 2 * HEAD * heads
        return pl.pallas_call(
            functools.partial(outgoing_kernel, *shape, base),
            in_specs=[SMEM, SMEM, VMEM],
            out_specs=VMEM,
            out_shape=jax.ShapeDtypeStruct((devices, slice_rows, 2 * HEAD * heads), BF16),
            scratch_shapes=[pltpu.VMEM((slice_rows, width), BF16)],
            compiler_params=params,
            name="outgoing_rows",
        )(member_list, prompt_slot, pool)

    def totals(base, block, others):
        held = [] if others is None else [others]
        return pl.pallas_call(
            functools.partial(total_kernel, *shape, base),
            in_specs=[SMEM, SMEM, VMEM] + [VMEM] * len(held),
            out_specs=VMEM,
            out_shape=jax.ShapeDtypeStruct(prefix_pool.shape, BF16),
            compiler_params=params,
            name="prefix_totals",
        )(member_list, prompt_slot, block, *held)

    own_kv = resp_kv.reshape(responses, rows, 2 * kv_width)
    prefix, _ = exchange(outgoing(*chunks[0], prefix_pool), ())
    held, summed, arrived = [], None, None
    for k, (base, heads) in enumerate(chunks):
        last = k + 1 == len(chunks)
        if not last:
            ahead = outgoing(*chunks[k + 1], prefix_pool)
            coming, (prefix, own_kv) = exchange(ahead, (prefix, own_kv))
        prefix = prefix.reshape(devices * slice_rows, 2 * HEAD * heads)
        *held, far_grad = attention_grads(
            queries, grad_out, own_kv, prefix, resp_len, base, held
        )
        far_grad = far_grad.reshape(devices, slice_rows, 2 * HEAD * heads)
        if arrived is None:
            arrived, _ = exchange(far_grad, ())
        else:
            following, (arrived,) = exchange(far_grad, (arrived,))
            summed = totals(chunks[k - 1][0], arrived, summed)
            arrived = following
        if not last:
            prefix = coming
    attention, grad_queries, own_dkey, own_dvalue = held
    grad_resp_kv = jnp.stack([own_dkey, own_dvalue], axis=2)
    grad_prefix = totals(chunks[-1][0], arrived, summed)
    return attention, grad_queries, grad_resp_kv, grad_prefix


def solution(mesh):
    return jax.shard_map(
        on_device,
        mesh=mesh,
        in_specs=(
            P("dp", None, "tensor"),
            P("dp", None, None, "tensor"),
            P(("dp", "tensor"), None, None, None),
            P("dp", None, "tensor"),
            P(),
            P(),
            P("dp"),
        ),
        out_specs=(
            P("dp", None, "tensor"),
            P("dp", None, "tensor"),
            P("dp", None, None, "tensor"),
            P(("dp", "tensor"), None, None, None),
        ),
        check_vma=False,
    )
```

time: 104 us -> 102 us (0.981)
  Pallas kernels: 35.3 us -> 44.5 us
  starting transfers between devices: 34.3 us -> 26.7 us
  waiting for transfers between devices: 26.2 us -> 21.7 us
    pallas_call x2, Pallas kernels: 26.9 us -> 36.3 us  [attention_grads(): pl.pallas_call(functools.partial(attention_kernel, tile_rows, head_block,...]
    all_to_all x4, starting transfers between devices: 34.3 us -> 26.7 us  [exchange(): lax.all_to_all(block, EVERYONE, split_axis=0, concat_axis=0, tiled=True)]
    all_to_all x4, waiting for transfers between devices: 26.2 us -> 21.7 us  [exchange(): lax.all_to_all(block, EVERYONE, split_axis=0, concat_axis=0, tiled=True)]
  transfers between devices with their start and end apart: 4 -> 4, of which waited for: 4 -> 2; matrix products, arithmetic and copies ran while one was open for 6% -> 6% of each run, Pallas kernels for 30% -> 40%
where the time goes in v4:
time: 102 us; the launch traced here: 100 us
  Pallas kernels  44.5 us (44%)
  starting transfers between devices  26.7 us (26%)
  waiting for transfers between devices  21.7 us (21%)
  local copies, waits for them, and re-layouts  5.43 us (5%)
  other arithmetic  1.3 us (1%)
    pallas_call x2, Pallas kernels, attention_grads(): pl.pallas_call(functools.partial(attention_kernel, tile_rows, head_block,...  36.3 us
    all_to_all x4, starting transfers between devices, exchange(): lax.all_to_all(block, EVERYONE, split_axis=0, concat_axis=0, tiled=True)  26.7 us
    all_to_all x4, waiting for transfers between devices, exchange(): lax.all_to_all(block, EVERYONE, split_axis=0, concat_axis=0, tiled=True)  21.7 us
    pallas_call x2, Pallas kernels, outgoing(): pl.pallas_call(functools.partial(outgoing_kernel, *shape, base), in_specs...  4.24 us
    pallas_call x2, Pallas kernels, totals(): pl.pallas_call(functools.partial(total_kernel, *shape, base), in_specs=[S...  3.88 us
    unnamed x9, local copies, waits for them, and re-layouts  2.86 us
    reshape x1, local copies, waits for them, and re-layouts, on_device(): own_kv = resp_kv.reshape(responses, rows, 2 * kv_width)  2.57 us
  transfers between devices with their start and end apart: 4, of which 2 were waited for; matrix products, arithmetic and copies ran while one was open for 6% of the time, Pallas kernels for 40%

profile of v4, /device:TPU:1, one launch (start us, length us, event | category | flops | bytes accessed | tf_op | source)
XLA Modules:
  0.0 100.3 jit_solution(2990236542446422242)
XLA Ops:
  0.6 2.1 %outgoing_rows.3 = bf16[32,16,512]{2,1,0:T(8,128)(2,1)} custom-call(s32[2,8]{1,0:T(2,128)} %member_ref.7, s32[2]{0:T(128)} %slot_ref.7, bf16[16,2,2,1024]{3,2,1,0:T(2,128)(2,1)} %pool_ref.3), custom_call_target="tpu_custom_call" | custom-call | tf_op jit(solution)/shard_map/outgoing_rows/pallas_call | solution.py:287
  2.7 7.1 %all-to-all-start = ((bf16[32,16,512]{2,1,0:T(8,128)(2,1)}), bf16[32,16,512]{2,1,0:T(8,128)(2,1)S(1)}, u32[]{:S(2)}, u32[]{:S(2)}) async-start(bf16[32,16,512]{2,1,0:T(8,128)(2,1)} %outgoing_rows.3), calls=%async_computation | async-start | bytes 1048576 | tf_op jit(solution)/shard_map/all_to_all | solution.py:265
  9.8 2.1 %outgoing_rows.2 = bf16[32,16,512]{2,1,0:T(8,128)(2,1)} custom-call(s32[2,8]{1,0:T(2,128)} %member_ref.7, s32[2]{0:T(128)} %slot_ref.7, bf16[16,2,2,1024]{3,2,1,0:T(2,128)(2,1)} %pool_ref.3), custom_call_target="tpu_custom_call" | custom-call | tf_op jit(solution)/shard_map/outgoing_rows/pallas_call | solution.py:287
  12.0 2.6 %reshape.23.refs_4_.refs_5_ = bf16[2,256,1024]{2,1,0:T(8,128)(2,1)} reshape(bf16[2,256,2,512]{3,2,1,0:T(2,128)(2,1)} %param.8) | data formatting | bytes 2097152 | tf_op jit(solution)/shard_map/reshape | solution.py:308
  14.5 11.1 %all-to-all-done = bf16[32,16,512]{2,1,0:T(8,128)(2,1)S(1)} async-done(((bf16[32,16,512]{2,1,0:T(8,128)(2,1)}), bf16[32,16,512]{2,1,0:T(8,128)(2,1)S(1)}, u32[]{:S(2)}, u32[]{:S(2)}) %all-to-all-start) | async-done | bytes 524320 | tf_op jit(solution)/shard_map/all_to_all | solution.py:265
  25.7 0.0 copy-start.3
  25.7 2.8 %all-to-all-start.1 = ((bf16[32,16,512]{2,1,0:T(8,128)(2,1)}), bf16[32,16,512]{2,1,0:T(8,128)(2,1)S(1)}, u32[]{:S(2)}, u32[]{:S(2)}) async-start(bf16[32,16,512]{2,1,0:T(8,128)(2,1)} %outgoing_rows.2), calls=%async_computation.1 | async-start | bytes 1048576 | tf_op jit(solution)/shard_map/all_to_all | solution.py:265
  28.5 0.0 copy-done.3
  28.5 18.1 %attention_grads.2 = (bf16[2,256,4096]{2,1,0:T(8,128)(2,1)}, bf16[2,256,4096]{2,1,0:T(8,128)(2,1)}, bf16[2,256,512]{2,1,0:T(8,128)(2,1)}, bf16[2,256,512]{2,1,0:T(8,128)(2,1)}, bf16[512,512]{1,0:T(8,128)(2,1)}) custom-call(s32[2]{0:T(128)} %refs_0_.3, bf16[2,256,4096]{2,1,0:T(8,128)(2,1)} %refs_1_.3, bf16[2,256,4096]{2,1,0:T(8,128)(2,1)} %refs_2_.3, ...), custom_call_target="tpu_custom_call" | custom-call | flops 9663676416 | bytes 8388608 | tf_op jit(solution)/shard_map/attention_grads/pallas_call | solution.py:182
  46.6 0.0 all-to-all-done.1
  46.6 0.0 copy-start.2
  46.6 8.4 %all-to-all-start.2 = ((bf16[32,16,512]{2,1,0:T(8,128)(2,1)}), bf16[32,16,512]{2,1,0:T(8,128)(2,1)S(1)}, u32[]{:S(2)}, u32[]{:S(2)}) async-start(bf16[32,16,512]{2,1,0:T(8,128)(2,1)} %bitcast.8), calls=%async_computation.2 | async-start | bytes 1048576 | tf_op jit(solution)/shard_map/all_to_all | solution.py:265
  55.0 0.0 copy-done.2
  55.0 18.3 %attention_grads.3 = (bf16[2,256,4096]{2,1,0:T(8,128)(2,1)}, bf16[2,256,4096]{2,1,0:T(8,128)(2,1)}, bf16[2,256,512]{2,1,0:T(8,128)(2,1)}, bf16[2,256,512]{2,1,0:T(8,128)(2,1)}, bf16[512,512]{1,0:T(8,128)(2,1)}) custom-call(s32[2]{0:T(128)} %refs_0_.3, ...), custom_call_target="tpu_custom_call", output_to_operand_aliasing={{0}: (6, {}), {1}: (7, {}), {2}: (8, {}), {3}: (9, {})} | custom-call | flops 9663676416 | bytes 8388608 | tf_op jit(solution)/shard_map/attention_grads/pallas_call | solution.py:182
  73.3 0.0 all-to-all-done.2.in_ref
  73.3 0.0 copy-start
  73.3 8.4 %all-to-all-start.3 = ((bf16[32,16,512]{2,1,0:T(8,128)(2,1)}), bf16[32,16,512]{2,1,0:T(8,128)(2,1)S(1)}, u32[]{:S(2)}, u32[]{:S(2)}) async-start(bf16[32,16,512]{2,1,0:T(8,128)(2,1)} %bitcast.7), calls=%async_computation.3 | async-start | bytes 1048576 | tf_op jit(solution)/shard_map/all_to_all | solution.py:265
  81.7 0.0 copy-done
  81.7 1.9 %prefix_totals.2.refs_0_ = bf16[16,2,2,1024]{3,2,1,0:T(2,128)(2,1)} custom-call(s32[2,8]{1,0:T(2,128)} %member_ref.7, s32[2]{0:T(128)} %slot_ref.7, bf16[32,16,512]{2,1,0:T(8,128)(2,1)} %copy-done), custom_call_target="tpu_custom_call" | custom-call | tf_op jit(solution)/shard_map/prefix_totals/pallas_call | solution.py:299
  83.6 1.3 %pad_maximum_fusion = bf16[2,256,2,512]{3,1,0,2:T(8,128)(2,1)S(1)} fusion(bf16[2,256,1,512]{3,1,0,2:T(8,128)(2,1)} %bitcast.11, bf16[2,256,1,512]{3,1,0,2:T(8,128)(2,1)} %bitcast.10), kind=kLoop, calls=%fused_computation | loop fusion | flops 524288 | bytes 2097152 | tf_op jit(solution)/shard_map/stack | solution.py:330
  84.9 2.0 %copy.15 = bf16[2,256,2,512]{3,2,1,0:T(2,128)(2,1)} copy(bf16[2,256,2,512]{3,1,0,2:T(8,128)(2,1)S(1)} %pad_maximum_fusion) | data formatting | bytes 2097152
  87.0 10.5 %all-to-all-done.3.in_ref = bf16[32,16,512]{2,1,0:T(8,128)(2,1)S(1)} async-done(((bf16[32,16,512]{2,1,0:T(8,128)(2,1)}), bf16[32,16,512]{2,1,0:T(8,128)(2,1)S(1)}, u32[]{:S(2)}, u32[]{:S(2)}) %all-to-all-start.3) | async-done | bytes 524320 | tf_op jit(solution)/shard_map/all_to_all | solution.py:265
  97.5 0.0 copy-start.1
  97.5 0.8 copy-done.1
  98.3 2.0 %prefix_totals.3 = bf16[16,2,2,1024]{3,2,1,0:T(2,128)(2,1)} custom-call(s32[2,8]{1,0:T(2,128)} %member_ref.7, s32[2]{0:T(128)} %slot_ref.7, bf16[32,16,512]{2,1,0:T(8,128)(2,1)} %copy-done.1, bf16[16,2,2,1024]{3,2,1,0:T(2,128)(2,1)} %prefix_totals.2.refs_0_), custom_call_target="tpu_custom_call" | custom-call | tf_op jit(solution)/shard_map/prefix_totals/pallas_call | solution.py:299
Async XLA Ops:
  2.7 22.9 %all-to-all-start = ((bf16[32,16,512]{2,1,0:T(8,128)(2,1)}), bf16[32,16,512]{2,1,0:T(8,128)(2,1)S(1)}, u32[]{:S(2)}, u32[]{:S(2)}) async-start(bf16[32,16,512]{2,1,0:T(8,128)(2,1)} %outgoing_rows.3), calls=%async_computation | async-start | bytes 1048576 | tf_op jit(solution)/shard_map/all_to_all | solution.py:265
  25.7 2.8 %copy-start.3 = (bf16[32,16,512]{2,1,0:T(8,128)(2,1)}, bf16[32,16,512]{2,1,0:T(8,128)(2,1)S(1)}, u32[]{:S(2)}) copy-start(bf16[32,16,512]{2,1,0:T(8,128)(2,1)S(1)} %all-to-all-done) | copy-start | bytes 1572868
  25.7 20.9 %all-to-all-start.1 = ((bf16[32,16,512]{2,1,0:T(8,128)(2,1)}), bf16[32,16,512]{2,1,0:T(8,128)(2,1)S(1)}, u32[]{:S(2)}, u32[]{:S(2)}) async-start(bf16[32,16,512]{2,1,0:T(8,128)(2,1)} %outgoing_rows.2), calls=%async_computation.1 | async-start | bytes 1048576 | tf_op jit(solution)/shard_map/all_to_all | solution.py:265
  46.6 8.4 %copy-start.2 = (bf16[32,16,512]{2,1,0:T(8,128)(2,1)}, bf16[32,16,512]{2,1,0:T(8,128)(2,1)S(1)}, u32[]{:S(2)}) copy-start(bf16[32,16,512]{2,1,0:T(8,128)(2,1)S(1)} %all-to-all-done.1) | copy-start | bytes 1572868
  46.6 26.7 %all-to-all-start.2 = ((bf16[32,16,512]{2,1,0:T(8,128)(2,1)}), bf16[32,16,512]{2,1,0:T(8,128)(2,1)S(1)}, u32[]{:S(2)}, u32[]{:S(2)}) async-start(bf16[32,16,512]{2,1,0:T(8,128)(2,1)} %bitcast.8), calls=%async_computation.2 | async-start | bytes 1048576 | tf_op jit(solution)/shard_map/all_to_all | solution.py:265
  73.3 8.4 %copy-start = (bf16[32,16,512]{2,1,0:T(8,128)(2,1)}, bf16[32,16,512]{2,1,0:T(8,128)(2,1)S(1)}, u32[]{:S(2)}) copy-start(bf16[32,16,512]{2,1,0:T(8,128)(2,1)S(1)} %all-to-all-done.2.in_ref) | copy-start | bytes 1572868
  73.3 24.2 %all-to-all-start.3 = ((bf16[32,16,512]{2,1,0:T(8,128)(2,1)}), bf16[32,16,512]{2,1,0:T(8,128)(2,1)S(1)}, u32[]{:S(2)}, u32[]{:S(2)}) async-start(bf16[32,16,512]{2,1,0:T(8,128)(2,1)} %bitcast.7), calls=%async_computation.3 | async-start | bytes 1048576 | tf_op jit(solution)/shard_map/all_to_all | solution.py:265
  97.5 0.8 copy-start.1

commit v5 on v4

--- a/solution.py
+++ b/solution.py
@@ -110,8 +110,8 @@
                 "first_row": t,
                 "count": prompt_rows + t + tile_rows,
             }
+            for t in reversed(tiles)
             for r in which
-            for t in reversed(tiles)
             for h in range(blocks)
         ]
         for step in range(len(stages) + len(chains) - 1):
@@ -219,11 +219,11 @@
         for t in range(tensor_count):
             source = (t * kv_local + base) * HEAD
             for h in range(heads):
+                place = source + h * HEAD
+                pair = pool_ref[:, slot, :, place : place + HEAD].astype(F32)
                 for part in range(2):
                     target = (slot * tensor_count + t) * width + (2 * h + part) * HEAD
-                    flat[:, target : target + HEAD] = pool_ref[
-                        :, slot, part, source + h * HEAD : source + (h + 1) * HEAD
-                    ]
+                    flat[:, target : target + HEAD] = pair[:, part, :].astype(BF16)
 
     def one(i, carry):
         prompt = i // members
@@ -248,13 +248,12 @@
             total = in_ref[member_ref[prompt, 0] * tensor_count + t].astype(F32)
             for m in range(1, members):
                 total += in_ref[member_ref[prompt, m] * tensor_count + t].astype(F32)
-            total = total.astype(BF16)
             for h in range(heads):
-                for part in range(2):
-                    target = (t * kv_local + base + h) * HEAD
-                    out_ref[:, slot_ref[prompt], part, target : target + HEAD] = total[
-                        :, (2 * h + part) * HEAD : (2 * h + part + 1) * HEAD
-                    ]
+                target = (t * kv_local + base + h) * HEAD
+                parts = [total[:, (2 * h + p) * HEAD : (2 * h + p + 1) * HEAD] for p in range(2)]
+                out_ref[:, slot_ref[prompt], :, target : target + HEAD] = jnp.stack(
+                    parts, axis=1
+                ).astype(BF16)
         return carry
 
     lax.fori_loop(0, prompts, one, 0)
@@ -266,7 +265,7 @@
 
 
 SMEM = pl.BlockSpec(memory_space=pltpu.SMEM)
-VMEM = pl.BlockSpec(memory_space=pltpu.VMEM)
+VMEM = pl.BlockSpec()
 
 
 def on_device(queries, resp_kv, prefix_pool, grad_out, member_list, prompt_slot, resp_len):

time: 102 us -> 104 us (1.020)
  starting transfers between devices: 26.7 us -> 29.4 us
    all_to_all x4, starting transfers between devices: 26.7 us -> 29.4 us  [exchange(): lax.all_to_all(block, EVERYONE, split_axis=0, concat_axis=0, tiled=True)]
  transfers between devices with their start and end apart: 4 -> 4, of which waited for: 2 -> 2; matrix products, arithmetic and copies ran while one was open for 6% -> 6% of each run, Pallas kernels for 40% -> 39%
where the time goes in v5:
time: 104 us; the launch traced here: 103 us
  Pallas kernels  44.3 us (43%)
  starting transfers between devices  29.4 us (28%)
  waiting for transfers between devices  21.8 us (21%)
  local copies, waits for them, and re-layouts  5.43 us (5%)
  other arithmetic  1.3 us (1%)
    pallas_call x2, Pallas kernels, attention_grads(): pl.pallas_call(functools.partial(attention_kernel, tile_rows, head_block,...  36.3 us
    all_to_all x4, starting transfers between devices, exchange(): lax.all_to_all(block, EVERYONE, split_axis=0, concat_axis=0, tiled=True)  29.4 us
    all_to_all x4, waiting for transfers between devices, exchange(): lax.all_to_all(block, EVERYONE, split_axis=0, concat_axis=0, tiled=True)  21.8 us
    pallas_call x2, Pallas kernels, outgoing(): pl.pallas_call(functools.partial(outgoing_kernel, *shape, base), in_specs...  4.1 us
    pallas_call x2, Pallas kernels, totals(): pl.pallas_call(functools.partial(total_kernel, *shape, base), in_specs=[S...  3.85 us
    unnamed x9, local copies, waits for them, and re-layouts  2.86 us
    reshape x1, local copies, waits for them, and re-layouts, on_device(): own_kv = resp_kv.reshape(responses, rows, 2 * kv_width)  2.57 us
  transfers between devices with their start and end apart: 4, of which 2 were waited for; matrix products, arithmetic and copies ran while one was open for 6% of the time, Pallas kernels for 39%

profile of v5, /device:TPU:1, one launch (start us, length us, event | category | flops | bytes accessed | tf_op | source)
XLA Modules:
  0.0 102.9 jit_solution(14835296743627566128)
XLA Ops:
  0.6 2.0 %outgoing_rows.3 = bf16[32,16,512]{2,1,0:T(8,128)(2,1)} custom-call(s32[2,8]{1,0:T(2,128)} %member_ref.7, s32[2]{0:T(128)} %slot_ref.7, bf16[16,2,2,1024]{3,2,1,0:T(2,128)(2,1)} %pool_ref.3), custom_call_target="tpu_custom_call" | custom-call | tf_op jit(solution)/shard_map/outgoing_rows/pallas_call | solution.py:286
  2.7 7.1 %all-to-all-start = ((bf16[32,16,512]{2,1,0:T(8,128)(2,1)}), bf16[32,16,512]{2,1,0:T(8,128)(2,1)S(1)}, u32[]{:S(2)}, u32[]{:S(2)}) async-start(bf16[32,16,512]{2,1,0:T(8,128)(2,1)} %outgoing_rows.3), calls=%async_computation | async-start | bytes 1048576 | tf_op jit(solution)/shard_map/all_to_all | solution.py:264
  9.8 2.1 %outgoing_rows.2 = bf16[32,16,512]{2,1,0:T(8,128)(2,1)} custom-call(s32[2,8]{1,0:T(2,128)} %member_ref.7, s32[2]{0:T(128)} %slot_ref.7, bf16[16,2,2,1024]{3,2,1,0:T(2,128)(2,1)} %pool_ref.3), custom_call_target="tpu_custom_call" | custom-call | tf_op jit(solution)/shard_map/outgoing_rows/pallas_call | solution.py:286
  11.8 2.6 %reshape.23.refs_4_.refs_5_ = bf16[2,256,1024]{2,1,0:T(8,128)(2,1)} reshape(bf16[2,256,2,512]{3,2,1,0:T(2,128)(2,1)} %param.8) | data formatting | bytes 2097152 | tf_op jit(solution)/shard_map/reshape | solution.py:307
  14.4 11.2 %all-to-all-done = bf16[32,16,512]{2,1,0:T(8,128)(2,1)S(1)} async-done(((bf16[32,16,512]{2,1,0:T(8,128)(2,1)}), bf16[32,16,512]{2,1,0:T(8,128)(2,1)S(1)}, u32[]{:S(2)}, u32[]{:S(2)}) %all-to-all-start) | async-done | bytes 524320 | tf_op jit(solution)/shard_map/all_to_all | solution.py:264
  25.6 0.0 copy-start.3
  25.6 2.8 %all-to-all-start.1 = ((bf16[32,16,512]{2,1,0:T(8,128)(2,1)}), bf16[32,16,512]{2,1,0:T(8,128)(2,1)S(1)}, u32[]{:S(2)}, u32[]{:S(2)}) async-start(bf16[32,16,512]{2,1,0:T(8,128)(2,1)} %outgoing_rows.2), calls=%async_computation.1 | async-start | bytes 1048576 | tf_op jit(solution)/shard_map/all_to_all | solution.py:264
  28.4 0.0 copy-done.3
  28.4 18.1 %attention_grads.2 = (bf16[2,256,4096]{2,1,0:T(8,128)(2,1)}, bf16[2,256,4096]{2,1,0:T(8,128)(2,1)}, bf16[2,256,512]{2,1,0:T(8,128)(2,1)}, bf16[2,256,512]{2,1,0:T(8,128)(2,1)}, bf16[512,512]{1,0:T(8,128)(2,1)}) custom-call(s32[2]{0:T(128)} %refs_0_.3, bf16[2,256,4096]{2,1,0:T(8,128)(2,1)} %refs_1_.3, bf16[2,256,4096]{2,1,0:T(8,128)(2,1)} %refs_2_.3, ...), custom_call_target="tpu_custom_call" | custom-call | flops 9663676416 | bytes 8388608 | tf_op jit(solution)/shard_map/attention_grads/pallas_call | solution.py:182
  46.5 0.0 all-to-all-done.1
  46.5 0.0 copy-start.2
  46.5 9.8 %all-to-all-start.2 = ((bf16[32,16,512]{2,1,0:T(8,128)(2,1)}), bf16[32,16,512]{2,1,0:T(8,128)(2,1)S(1)}, u32[]{:S(2)}, u32[]{:S(2)}) async-start(bf16[32,16,512]{2,1,0:T(8,128)(2,1)} %bitcast.8), calls=%async_computation.2 | async-start | bytes 1048576 | tf_op jit(solution)/shard_map/all_to_all | solution.py:264
  56.3 0.0 copy-done.2
  56.3 18.3 %attention_grads.3 = (bf16[2,256,4096]{2,1,0:T(8,128)(2,1)}, bf16[2,256,4096]{2,1,0:T(8,128)(2,1)}, bf16[2,256,512]{2,1,0:T(8,128)(2,1)}, bf16[2,256,512]{2,1,0:T(8,128)(2,1)}, bf16[512,512]{1,0:T(8,128)(2,1)}) custom-call(s32[2]{0:T(128)} %refs_0_.3, ...), custom_call_target="tpu_custom_call", output_to_operand_aliasing={{0}: (6, {}), {1}: (7, {}), {2}: (8, {}), {3}: (9, {})} | custom-call | flops 9663676416 | bytes 8388608 | tf_op jit(solution)/shard_map/attention_grads/pallas_call | solution.py:182
  74.5 0.0 all-to-all-done.2.in_ref
  74.5 0.0 copy-start
  74.6 9.8 %all-to-all-start.3 = ((bf16[32,16,512]{2,1,0:T(8,128)(2,1)}), bf16[32,16,512]{2,1,0:T(8,128)(2,1)S(1)}, u32[]{:S(2)}, u32[]{:S(2)}) async-start(bf16[32,16,512]{2,1,0:T(8,128)(2,1)} %bitcast.7), calls=%async_computation.3 | async-start | bytes 1048576 | tf_op jit(solution)/shard_map/all_to_all | solution.py:264
  84.3 0.0 copy-done
  84.4 1.9 %prefix_totals.2.refs_0_ = bf16[16,2,2,1024]{3,2,1,0:T(2,128)(2,1)} custom-call(s32[2,8]{1,0:T(2,128)} %member_ref.7, s32[2]{0:T(128)} %slot_ref.7, bf16[32,16,512]{2,1,0:T(8,128)(2,1)} %copy-done), custom_call_target="tpu_custom_call" | custom-call | tf_op jit(solution)/shard_map/prefix_totals/pallas_call | solution.py:298
  86.3 1.3 %pad_maximum_fusion = bf16[2,256,2,512]{3,1,0,2:T(8,128)(2,1)S(1)} fusion(bf16[2,256,1,512]{3,1,0,2:T(8,128)(2,1)} %bitcast.11, bf16[2,256,1,512]{3,1,0,2:T(8,128)(2,1)} %bitcast.10), kind=kLoop, calls=%fused_computation | loop fusion | flops 524288 | bytes 2097152 | tf_op jit(solution)/shard_map/stack | solution.py:329
  87.6 2.0 %copy.15 = bf16[2,256,2,512]{3,2,1,0:T(2,128)(2,1)} copy(bf16[2,256,2,512]{3,1,0,2:T(8,128)(2,1)S(1)} %pad_maximum_fusion) | data formatting | bytes 2097152
  89.6 10.6 %all-to-all-done.3.in_ref = bf16[32,16,512]{2,1,0:T(8,128)(2,1)S(1)} async-done(((bf16[32,16,512]{2,1,0:T(8,128)(2,1)}), bf16[32,16,512]{2,1,0:T(8,128)(2,1)S(1)}, u32[]{:S(2)}, u32[]{:S(2)}) %all-to-all-start.3) | async-done | bytes 524320 | tf_op jit(solution)/shard_map/all_to_all | solution.py:264
  100.2 0.0 copy-start.1
  100.2 0.8 copy-done.1
  101.0 1.9 %prefix_totals.3 = bf16[16,2,2,1024]{3,2,1,0:T(2,128)(2,1)} custom-call(s32[2,8]{1,0:T(2,128)} %member_ref.7, s32[2]{0:T(128)} %slot_ref.7, bf16[32,16,512]{2,1,0:T(8,128)(2,1)} %copy-done.1, bf16[16,2,2,1024]{3,2,1,0:T(2,128)(2,1)} %prefix_totals.2.refs_0_), custom_call_target="tpu_custom_call" | custom-call | tf_op jit(solution)/shard_map/prefix_totals/pallas_call | solution.py:298
Async XLA Ops:
  2.7 22.9 %all-to-all-start = ((bf16[32,16,512]{2,1,0:T(8,128)(2,1)}), bf16[32,16,512]{2,1,0:T(8,128)(2,1)S(1)}, u32[]{:S(2)}, u32[]{:S(2)}) async-start(bf16[32,16,512]{2,1,0:T(8,128)(2,1)} %outgoing_rows.3), calls=%async_computation | async-start | bytes 1048576 | tf_op jit(solution)/shard_map/all_to_all | solution.py:264
  25.6 2.8 %copy-start.3 = (bf16[32,16,512]{2,1,0:T(8,128)(2,1)}, bf16[32,16,512]{2,1,0:T(8,128)(2,1)S(1)}, u32[]{:S(2)}) copy-start(bf16[32,16,512]{2,1,0:T(8,128)(2,1)S(1)} %all-to-all-done) | copy-start | bytes 1572868
  25.6 20.9 %all-to-all-start.1 = ((bf16[32,16,512]{2,1,0:T(8,128)(2,1)}), bf16[32,16,512]{2,1,0:T(8,128)(2,1)S(1)}, u32[]{:S(2)}, u32[]{:S(2)}) async-start(bf16[32,16,512]{2,1,0:T(8,128)(2,1)} %outgoing_rows.2), calls=%async_computation.1 | async-start | bytes 1048576 | tf_op jit(solution)/shard_map/all_to_all | solution.py:264
  46.5 9.8 %copy-start.2 = (bf16[32,16,512]{2,1,0:T(8,128)(2,1)}, bf16[32,16,512]{2,1,0:T(8,128)(2,1)S(1)}, u32[]{:S(2)}) copy-start(bf16[32,16,512]{2,1,0:T(8,128)(2,1)S(1)} %all-to-all-done.1) | copy-start | bytes 1572868
  46.5 28.1 %all-to-all-start.2 = ((bf16[32,16,512]{2,1,0:T(8,128)(2,1)}), bf16[32,16,512]{2,1,0:T(8,128)(2,1)S(1)}, u32[]{:S(2)}, u32[]{:S(2)}) async-start(bf16[32,16,512]{2,1,0:T(8,128)(2,1)} %bitcast.8), calls=%async_computation.2 | async-start | bytes 1048576 | tf_op jit(solution)/shard_map/all_to_all | solution.py:264
  74.5 9.8 %copy-start = (bf16[32,16,512]{2,1,0:T(8,128)(2,1)}, bf16[32,16,512]{2,1,0:T(8,128)(2,1)S(1)}, u32[]{:S(2)}) copy-start(bf16[32,16,512]{2,1,0:T(8,128)(2,1)S(1)} %all-to-all-done.2.in_ref) | copy-start | bytes 1572868
  74.6 25.6 %all-to-all-start.3 = ((bf16[32,16,512]{2,1,0:T(8,128)(2,1)}), bf16[32,16,512]{2,1,0:T(8,128)(2,1)S(1)}, u32[]{:S(2)}, u32[]{:S(2)}) async-start(bf16[32,16,512]{2,1,0:T(8,128)(2,1)} %bitcast.7), calls=%async_computation.3 | async-start | bytes 1048576 | tf_op jit(solution)/shard_map/all_to_all | solution.py:264
  100.2 0.8 copy-start.1
